TPU v7x, 32 devices: a whole 2x2x4 slice. The times are simulated.
32 devices in a mesh: dp: 8 (over y, x, core), mp: 4 (over z).
Axes of the slice: x: 2, y: 2, z: 4, core: 2. Of those that a mesh axis runs over, the one named last changes fastest.
Arguments:
- tokens: bfloat16 [8192, 6144], P('dp', 'mp'), may hold values from -6 to 6
- dest_pos: int32 [8192], P('dp'), may hold values from 0 to 8191, as said below
- src_row: int32 [8192], P('dp'), may hold values from 0 to 8191, as said below
- segment_ids: int32 [8192], P('dp'), may hold values from 0 to 7, as said below
- norm_gain: float32 [6144], replicated, may hold values from 0.1 to 1.9
- qkv_weight: bfloat16 [3, 6144, 3072], P(None, None, 'mp'), may hold values from -0.078125 to 0.078125
- qk_gain: float32 [2, 24, 128], P(None, 'mp'), may hold values from 0.5 to 12
- out_weight: bfloat16 [3072, 6144], P('mp'), may hold values from -0.109375 to 0.109375
Outputs:
- updated: bfloat16 [8192, 6144], P('dp', 'mp')
Inputs may be any that keep to these rules, and one draw needn't show every extreme that they name: `dest_pos`: each index of dp holds 1024 image rows and sends one contiguous block of whole patch rows (16 rows each) to every sequence, the rows keeping their order there; the block sizes of one index of dp are the same numbers for every index, in another order, the largest exactly 192; every sequence receives one block of each size, in a drawn order; each position is named once. `src_row`: the inverse of dest_pos. `segment_ids`: the index of the received block that a position lies in, counted within its sequence; never falling along a sequence.
All inputs are finite; a program needn't handle non-finite values.
Results may differ from a plain program's by a relative error of at most 0.012.
The roundings to bfloat16 on the way count: a program that leaves them out, or rounds other values in their place, can miss the bound.
Values may be sent and summed in bfloat16 or wider, within the bound.
No kernel may reach another device: no remote copies, remote signals or barrier semaphores. Data moves between devices by JAX's collectives and lax.ppermute only.
A program may use at most 192 MiB of HBM per device.

v0:
```python
import functools
import math

import jax
import jax.numpy as jnp
import numpy as np
from jax import lax
from jax.experimental import pallas as pl
from jax.experimental.pallas import tpu as pltpu
from jax.sharding import PartitionSpec as P

HEAD_DIM = 128
EPS = 1e-06
NEG = -1e30
VMEM = 56 * 1024 * 1024
COST = pl.CostEstimate(flops=15 * 10**9, bytes_accessed=2**20, transcendentals=0)


def pick(total, wanted):
    return max(w for w in range(128, min(total, wanted) + 1, 128) if total % w == 0)


def line_schedule(n):
    steps = {}
    for s in range(1, n):
        for kind, low in (("E", 0), ("O", 1)):
            pairs = []
            for i in range(low, n - 1, 2):
                if i - s + 1 >= 0:
                    pairs.append((i, i + 1))
                if i + s <= n - 1:
                    pairs.append((i + 1, i))
            if pairs:
                steps[(s, kind)] = pairs
    slots = [[] for _ in range(n)]
    for (s, kind), pairs in sorted(steps.items()):
        for source, target in pairs:
            origin = target - s if source < target else target + s
            slots[target].append(((s, kind), origin))
    return steps, slots


class Relay:
    def __init__(self, block, axis, n):
        self.axis, self.n = axis, n
        self.steps, self.slots = line_schedule(n)
        self.got = {(0, "E"): block, (0, "O"): block}

    def step(self, s, *after):
        kinds = [kind for kind in "EO" if (s, kind) in self.steps]
        sources = [self.got[(s - 1, "O" if kind == "E" else "E")] for kind in kinds]
        tied = lax.optimization_barrier((*sources, *after))
        for kind, source in zip(kinds, tied):
            self.got[(s, kind)] = lax.ppermute(source, self.axis, self.steps[(s, kind)])
        return tied[len(kinds) : len(kinds) + len(after)]

    def arrived(self, k):
        keys = sorted({slot[k][0] for slot in self.slots})
        if all({key for key, _ in slot} & set(keys) == {slot[k][0]} for slot in self.slots):
            return [self.got[key] for key in keys]
        place = lax.axis_index(self.axis)
        value = self.got[keys[0]]
        for key in keys[1:]:
            here = np.array([slot[k][0] == key for slot in self.slots])
            value = jnp.where(jnp.asarray(here)[place], self.got[key], value)
        return [value]


def origins(axis, n):
    _, slots = line_schedule(n)
    table = np.array([[slots[i][k][1] for k in range(n - 1)] for i in range(n)], np.int32)
    place = lax.axis_index(axis)
    return [jnp.asarray(table)[place, k] for k in range(n - 1)]


def whole(refs):
    value = refs[0][...]
    for ref in refs[1:]:
        value = value + ref[...]
    return value


def normalize(refs, average_ref, inverse_ref, gain_ref):
    centred = whole(refs).astype(jnp.float32) - average_ref[...]
    return (centred * inverse_ref[...] * gain_ref[...]).astype(jnp.bfloat16)


def project(parts, norm, weight, which, acc):
    rows, depth = parts[0].shape
    kinds, _, width = weight.shape
    cols = pick(width, 768)
    count = len(parts)

    def kernel(which_ref, *refs):
        normed, out_ref = refs[-1], refs[-2]

        @pl.when((pl.program_id(0) == 0) & (pl.program_id(1) == 0))
        def _():
            normed[...] = normalize(refs[:count], *refs[count : count + 3])

        part = jnp.dot(normed[...], refs[count + 3][...], preferred_element_type=jnp.float32)
        if acc is not None:
            part = part + refs[count + 4][...]
        out_ref[...] = part

    tile = pl.BlockSpec((None, rows, cols), lambda c, j, w: (c, 0, j))
    in_specs = [pl.BlockSpec((rows, depth), lambda c, j, w: (0, 0)) for _ in parts]
    in_specs += [pl.BlockSpec((rows, 1), lambda c, j, w: (0, 0))] * 2
    in_specs.append(pl.BlockSpec((1, depth), lambda c, j, w: (0, w[0])))
    in_specs.append(pl.BlockSpec((None, depth, cols), lambda c, j, w: (c, w[0], j)))
    args = [jnp.reshape(which, (1,)), *parts, *norm, weight]
    aliases = {}
    if acc is not None:
        in_specs.append(tile)
        args.append(acc)
        aliases = {len(args) - 1: 0}
    return pl.pallas_call(
        kernel,
        grid_spec=pltpu.PrefetchScalarGridSpec(
            num_scalar_prefetch=1,
            grid=(kinds, width // cols),
            in_specs=in_specs,
            out_specs=tile,
            scratch_shapes=[pltpu.VMEM((rows, depth), jnp.bfloat16)],
        ),
        out_shape=jax.ShapeDtypeStruct((kinds, rows, width), jnp.float32),
        input_output_aliases=aliases,
        compiler_params=pltpu.CompilerParams(vmem_limit_bytes=VMEM),
        cost_estimate=pl.CostEstimate(
            flops=2 * kinds * rows * depth * width,
            bytes_accessed=2 * kinds * depth * width + 8 * kinds * rows * width,
            transcendentals=0,
        ),
    )(*args)


def head_norm(values, gain):
    average = jnp.mean(values, axis=-1, keepdims=True)
    centred = values - average
    variance = jnp.mean(centred * centred, axis=-1, keepdims=True)
    return (centred * lax.rsqrt(variance + EPS) * gain).astype(jnp.bfloat16)


def attend(parts, norm, weight, which, acc, gains, block_col, block_row, first, heads, reach):
    rows, depth = parts[0].shape
    kinds = weight.shape[0]
    cols = heads * HEAD_DIM
    deep = pick(depth, 512)
    steps = depth // deep
    tile = pick(rows, 256)
    scale = math.log2(math.e) / math.sqrt(HEAD_DIM)
    count = len(parts)

    def kernel(which_ref, *refs):
        norm_refs = refs[count : count + 3]
        x_refs, refs = refs[:count], refs[3:]
        w_refs = refs[count : count + kinds]
        acc_refs = refs[count + kinds : count + 2 * kinds]
        gain_ref, col_ref, row_ref, out_ref, held = refs[count + 2 * kinds :]
        step = pl.program_id(0)

        @pl.when(step == 0)
        def _():
            for c in range(kinds):
                held[c] = acc_refs[c][...]

        x = normalize(x_refs, *norm_refs)
        for c in range(kinds):
            held[c] += jnp.dot(x, w_refs[c][...], preferred_element_type=jnp.float32)

        def one_head(h, carry):
            at = pl.ds(pl.multiple_of(h * HEAD_DIM, HEAD_DIM), HEAD_DIM)
            gain = gain_ref[h]
            query = head_norm(held[0, :, at], gain[0:1, :])
            key = head_norm(held[1, :, at], gain[1:2, :])
            value = held[2, :, at].astype(jnp.bfloat16)
            for begin in range(0, rows, tile):
                low = max(0, (begin - reach) // 128 * 128)
                high = min(rows, -(-(begin + tile + reach) // 128) * 128)
                scores = lax.dot_general(
                    query[begin : begin + tile],
                    key[low:high],
                    (((1,), (1,)), ((), ())),
                    preferred_element_type=jnp.float32,
                )
                same = col_ref[begin : begin + tile, :] == row_ref[:, low:high]
                scores = jnp.where(same, scores, NEG)
                top = jnp.max(scores, axis=-1, keepdims=True)
                expo = jnp.exp2((scores - top) * scale)
                total = jnp.sum(expo, axis=-1, keepdims=True)
                weights = (expo * (1.0 / total)).astype(jnp.bfloat16)
                context = jnp.dot(weights, value[low:high], preferred_element_type=jnp.float32)
                out_ref[begin : begin + tile, at] = context.astype(jnp.bfloat16)
            return carry

        @pl.when(step == steps - 1)
        def _():
            lax.fori_loop(0, heads, one_head, 0)

    def w_spec(c):
        return pl.BlockSpec(
            (None, deep, cols), lambda s, w: (c, w[0] * steps + s, first // heads)
        )

    def acc_spec(c):
        return pl.BlockSpec((None, rows, cols), lambda s, w: (c, 0, first // heads))

    in_specs = [pl.BlockSpec((rows, deep), lambda s, w: (0, s)) for _ in parts]
    in_specs += [pl.BlockSpec((rows, 1), lambda s, w: (0, 0))] * 2
    in_specs.append(pl.BlockSpec((1, deep), lambda s, w: (0, w[0] * steps + s)))
    in_specs += [w_spec(c) for c in range(kinds)] + [acc_spec(c) for c in range(kinds)]
    in_specs += [
        pl.BlockSpec((heads, 2, HEAD_DIM), lambda s, w: (first // heads, 0, 0)),
        pl.BlockSpec((rows, 1), lambda s, w: (0, 0)),
        pl.BlockSpec((1, rows), lambda s, w: (0, 0)),
    ]
    return pl.pallas_call(
        kernel,
        grid_spec=pltpu.PrefetchScalarGridSpec(
            num_scalar_prefetch=1,
            grid=(steps,),
            in_specs=in_specs,
            out_specs=pl.BlockSpec((rows, cols), lambda s, w: (0, 0)),
            scratch_shapes=[pltpu.VMEM((kinds, rows, cols), jnp.float32)],
        ),
        out_shape=jax.ShapeDtypeStruct((rows, cols), jnp.bfloat16),
        compiler_params=pltpu.CompilerParams(vmem_limit_bytes=VMEM),
        cost_estimate=COST,
    )(
        jnp.reshape(which, (1,)), *parts, *norm, *([weight] * kinds), *([acc] * kinds),
        gains, block_col, block_row,
    )


def project_out(pieces, weight, which, acc, residual):
    rows = pieces[0][0].shape[0]
    _, depth, _ = weight.shape
    width = which[1]
    high = pick(rows, 256)
    flat = [array for piece in pieces for array in piece]

    def kernel(which_ref, *refs):
        out_ref = refs[-1]
        w_ref = refs[len(flat)]
        total = None if acc is None else refs[len(flat) + 1][...]
        first = begin = 0
        for piece in pieces:
            x = whole(refs[first : first + len(piece)])
            first += len(piece)
            part = jnp.dot(
                x, w_ref[begin : begin + x.shape[1], :], preferred_element_type=jnp.float32
            )
            begin += x.shape[1]
            total = part if total is None else total + part
        if residual is not None:
            total = refs[-2][...].astype(jnp.float32) + total
        out_ref[...] = total.astype(out_ref.dtype)

    tile = pl.BlockSpec((high, width), lambda i, w: (i, 0))
    in_specs = [pl.BlockSpec((high, p.shape[1]), lambda i, w: (i, 0)) for p in flat]
    in_specs.append(pl.BlockSpec((None, depth, width), lambda i, w: (w[0], 0, w[1])))
    args = [jnp.stack([which[0], which[2]]), *flat, weight]
    for extra in (acc, residual):
        if extra is not None:
            in_specs.append(tile)
            args.append(extra)
    out_type = jnp.float32 if residual is None else jnp.bfloat16
    return pl.pallas_call(
        kernel,
        grid_spec=pltpu.PrefetchScalarGridSpec(
            num_scalar_prefetch=1, grid=(rows // high,), in_specs=in_specs, out_specs=tile
        ),
        out_shape=jax.ShapeDtypeStruct((rows, width), out_type),
        compiler_params=pltpu.CompilerParams(vmem_limit_bytes=VMEM),
        cost_estimate=COST,
    )(*args)


def exchange_out_weight(out_weight, n, groups):
    depth, features = out_weight.shape
    place = lax.axis_index("mp")
    piece = depth // groups
    cols = features // n
    mine = lax.dynamic_slice_in_dim(out_weight, lax.axis_index("dp") * piece, piece, axis=0)

    def columns(index):
        return lax.dynamic_slice_in_dim(mine, index * cols, cols, axis=1)

    received = [(place, columns(place))]
    for d in range(1, n):
        sent = lax.ppermute(
            columns((place + d) % n), "mp", [(i, (i + d) % n) for i in range(n)]
        )
        received.append(((place - d) % n, sent))
    return received


def stack(received):
    pieces = jnp.zeros((len(received), *received[0][1].shape), received[0][1].dtype)
    for origin, array in received:
        pieces = lax.dynamic_update_slice_in_dim(pieces, array[None], origin, axis=0)
    return pieces


def shards(tokens, dest_pos, src_row, segment_ids, norm_gain, qkv_weight, qk_gain, out_weight):
    groups = lax.axis_size("dp")
    n = lax.axis_size("mp")
    place = lax.axis_index("mp")
    rows, cols = tokens.shape
    features = cols * n
    reach = 3 * rows // (2 * groups)
    heads = qkv_weight.shape[2] // HEAD_DIM

    segment = lax.all_gather(segment_ids, "dp", tiled=True)[dest_pos]
    block = dest_pos // rows * groups + segment
    block_col = block[:, None]
    block_row = block[None, :]
    gains = jnp.transpose(qk_gain, (1, 0, 2))

    with jax.named_scope("moments"):
        values = tokens.astype(jnp.float32)
        moments = jnp.stack([jnp.sum(values, axis=1), jnp.sum(values * values, axis=1)])
        sums = moments
        for d in range(1, n):
            sums = sums + lax.ppermute(moments, "mp", [(i, (i + d) % n) for i in range(n)])
        average = sums[0] / features
        variance = sums[1] / features - average * average
        inverse = lax.rsqrt(variance + EPS)
        norm = (average[:, None], inverse[:, None], norm_gain[None, :])

    sources = origins("mp", n)

    def step_project(parts, origin, acc):
        with jax.named_scope("project"):
            return project(parts, norm, qkv_weight, origin, acc)

    line = Relay(tokens, "mp", n)
    line.step(1, sums)
    projected = step_project([tokens], place, None)
    pieces = out_weight
    for s in range(2, n):
        there = [line.got[key] for key in line.steps if key[0] == s - 1]
        pieces = line.step(s, projected, block, pieces, *there)[2]
        if s == 2:
            pieces = stack(exchange_out_weight(pieces, n, groups))
        elif s == 3:
            out_columns = lax.all_gather(pieces, "dp", axis=1, tiled=True)
        projected = step_project(line.arrived(s - 2), sources[s - 2], projected)
    last = line.arrived(n - 2)

    chunk = 2 if heads % 2 == 0 else 1
    contexts, lines = [], []
    for first in range(0, heads, chunk):
        if contexts:
            before = [contexts[-1]]
            if len(lines) >= 2:
                before += [lines[-2].got[(1, kind)] for kind in "EO"]
            gains = lax.optimization_barrier((gains, *before))[0]
        with jax.named_scope("attend"):
            context = attend(
                last, norm, qkv_weight, sources[n - 2], projected, gains, block_col, block_row,
                first, chunk, reach,
            )
        contexts.append(context)
        lines.append(Relay(context, "mp", n))
        lines[-1].step(1)

    zero = jnp.zeros((), jnp.int32)

    def step_out(k, acc, residual):
        pieces = [line.arrived(k) for line in lines]
        return project_out(pieces, out_columns, (sources[k], cols, zero), acc, residual)

    lines[0].step(2)
    there = [lines[0].got[key] for key in lines[0].steps if key[0] == 2]
    tied = lax.optimization_barrier((*contexts, *there))[: len(contexts)]
    total = project_out([[c] for c in tied], out_weight[None], (zero, cols, place), None, None)
    for s in range(2, n):
        for line in lines:
            if line is lines[-1]:
                line.step(s, total)
            elif s > 2 or line is not lines[0]:
                line.step(s)
        total = step_out(s - 2, total, None)
    return step_out(n - 2, total, tokens)


def solution(mesh):
    in_specs = (
        P("dp", "mp"),
        P("dp"),
        P("dp"),
        P("dp"),
        P(),
        P(None, None, "mp"),
        P(None, "mp", None),
        P("mp", None),
    )
    out_specs = P("dp", "mp")
    return jax.shard_map(shards, mesh=mesh, in_specs=in_specs, out_specs=out_specs, check_vma=False)
```

profile of v0, /device:TPU:0, one launch (start us, length us, event | category | flops | bytes accessed | tf_op | source)
XLA Modules:
  0.0 392.5 jit_solution(5834263270317303998)
XLA Ops:
  6.5 3.1 convert_reduce_fusion
  9.6 3.1 collective-permute-start
  12.7 2.6 collective-permute-start.1
  15.3 1.3 collective-permute-start.2
  17.3 1.6 collective-permute-done.2
  19.0 2.4 collective-permute-start.3
  21.3 1.1 collective-permute-start.4
  22.4 9.1 %all_gather.6 = s32[8192]{0:T(1024)S(1)} all-gather(s32[1024]{0:T(1024)S(1)} %copy-done.4), channel_id=1, replica_groups=mesh['dp'=8,'mp'=4] {'dp'}, dimensions={0}, use_global_device_ids=true | all-gather | bytes 36864 | tf_op jit(solution)/shard_map/all_gather | solution.py:314
  31.5 6.1 %gather_fusion = s32[1024]{0:T(1024)S(1)} fusion(s32[8192]{0:T(1024)S(1)} %all_gather.6, s32[1024]{0:T(1024)S(1)} %fusion.4), kind=kCustom, calls=%fused_computation | custom fusion | bytes 12288 | tf_op jit(solution)/shard_map/gather | solution.py:314
  38.7 1.0 copy.36
  40.8 2.1 add_rsqrt_fusion.refs_2_.refs_3_
  42.9 13.6 %project.3.refs_5_ = f32[3,1024,768]{2,1,0:T(8,128)} custom-call(s32[1]{0:T(128)} %bitcast.3.which_ref, bf16[1024,1536]{1,0:T(8,128)(2,1)} %refs_8_.1, f32[1024,1]{1,0:T(8,128)} %copy.37.refs_1_.refs_2_, f32[1024,1]{1,0:T(8,128)} %add_rsqrt_fusion.refs_2_.refs_3_, f32[1,6144]{1,0:T(1,128)} %bitcast.25, bf16[3,6144,768]{2,1,0:T(8,128)(2,1)} %refs_7_.5), custom_call_target="tpu_custom_call" | custom-call | flops 7247757312 | bytes 25952256 | tf_op jit(solution)/shard_map/project/pallas_call | solution.py:117
  56.5 33.4 %collective-permute-done.4.refs_0_ = bf16[1024,1536]{1,0:T(8,128)(2,1)} collective-permute-done((bf16[1024,1536]{1,0:T(8,128)(2,1)S(1)}, bf16[1024,1536]{1,0:T(8,128)(2,1)}, u32[]{:S(2)}, u32[]{:S(2)}) %collective-permute-start.4) | collective-permute-done | bytes 3145760 | tf_op jit(solution)/shard_map/ppermute | solution.py:54
  90.7 1.3 collective-permute-start.9
  92.8 1.7 fusion.9
  94.5 4.9 %collective-permute-start.6 = (bf16[96,1536]{1,0:T(8,128)(2,1)S(1)}, bf16[96,1536]{1,0:T(8,128)(2,1)S(1)}, u32[]{:S(2)}, u32[]{:S(2)}) collective-permute-start(bf16[96,1536]{1,0:T(8,128)(2,1)S(1)} %get-tuple-element.59), channel_id=1, source_target_pairs={{0,1},{1,2},{2,3},{3,0},{4,5},{5,6},{6,7},{7,4},{8,9},{9,10},{10,1... | collective-permute-start | bytes 884744 | tf_op jit(solution)/shard_map/ppermute | solution.py:291
  100.2 2.8 collective-permute-start.8
  103.1 16.4 %project.4.refs_6_ = f32[3,1024,768]{2,1,0:T(8,128)} custom-call(s32[1]{0:T(128)} %bitcast.7.which_ref, bf16[1024,1536]{1,0:T(8,128)(2,1)} %collective-permute-done.4.refs_0_, f32[1024,1]{1,0:T(8,128)} %copy.37.refs_1_.refs_2_, f32[1024,1]{1,0:T(8,128)} %add_rsqrt_fusion.refs_2_.refs_3_, f32[1,6144]{1,0:T(1,128)} %bitcast.26, ...), custom_call_target="tpu_custom_call", output_to_operand_aliasing={{}: (6, {})} | custom-call | flops 7247757312 | bytes 25952256 | tf_op jit(solution)/shard_map/project/pallas_call | solution.py:117
  119.5 1.2 broadcast_in_dim.34
  120.7 1.9 bitcast_dynamic-update-slice_fusion.3
  123.3 58.2 %collective-permute-done.7 = bf16[96,1536]{1,0:T(8,128)(2,1)S(1)} collective-permute-done((bf16[96,1536]{1,0:T(8,128)(2,1)S(1)}, bf16[96,1536]{1,0:T(8,128)(2,1)S(1)}, u32[]{:S(2)}, u32[]{:S(2)}) %collective-permute-start.7) | collective-permute-done | bytes 294944 | tf_op jit(solution)/shard_map/ppermute | solution.py:291
  183.0 1.5 collective-permute-start.10
  184.5 1.0 copy.41.refs_12_
  186.1 1.3 pad_add_fusion.1.which_ref
  187.4 1.9 pad_add_fusion
  189.3 18.0 %project.5.refs_8_.refs_9_.refs_10_ = f32[3,1024,768]{2,1,0:T(8,128)} custom-call(s32[1]{0:T(128)} %bitcast.12.which_ref, bf16[1024,1536]{1,0:T(8,128)(2,1)} %collective-permute-done.3.refs_0_, bf16[1024,1536]{1,0:T(8,128)(2,1)} %collective-permute-done.9.refs_1_, f32[1024,1]{1,0:T(8,128)} %copy.37.refs_1_.refs_2_, ...), custom_call_target="tpu_custom_call", output_to_operand_aliasing={{}: (7, {})} | custom-call | flops 7247757312 | bytes 25952256 | tf_op jit(solution)/shard_map/project/pallas_call | solution.py:117
  207.4 44.9 %collective-permute-done.10.refs_1_ = bf16[1024,1536]{1,0:T(8,128)(2,1)} collective-permute-done((bf16[1024,1536]{1,0:T(8,128)(2,1)S(1)}, bf16[1024,1536]{1,0:T(8,128)(2,1)}, u32[]{:S(2)}, u32[]{:S(2)}) %collective-permute-start.10) | collective-permute-done | bytes 3145760 | tf_op jit(solution)/shard_map/ppermute | solution.py:54
  252.2 14.8 %attend.3.refs_0_ = bf16[1024,256]{1,0:T(8,128)(2,1)} custom-call(s32[1]{0:T(128)} %bitcast.which_ref, bf16[1024,1536]{1,0:T(8,128)(2,1)} %copy-done, bf16[1024,1536]{1,0:T(8,128)(2,1)} %collective-permute-done.10.refs_1_, f32[1024,1]{1,0:T(8,128)} %copy.37.refs_1_.refs_2_, f32[1024,1]{1,0:T(8,128)} %add_rsqrt_fusion.refs_2_.refs_3_, f32[1,6144]{1,0:T(1,128)} %bitcast.28, ...), custom_call_target="tpu_custom_call" | custom-call | flops 15000000512 | bytes 1048576 | tf_op jit(solution)/shard_map/attend/pallas_call | solution.py:217
  267.8 4.7 %collective-permute-start.12 = (bf16[1024,256]{1,0:T(8,128)(2,1)}, bf16[1024,256]{1,0:T(8,128)(2,1)S(1)}, u32[]{:S(2)}, u32[]{:S(2)}) collective-permute-start(bf16[1024,256]{1,0:T(8,128)(2,1)} %attend.3.refs_0_), channel_id=1, source_target_pairs={{0,1},{1,0},{2,3},{3,2},{4,5},{5,4},{6,7},{7,6},{8,9},{9,8},{10,11... | collective-permute-start | bytes 1572872 | tf_op jit(solution)/shard_map/ppermute | solution.py:54
  272.5 14.8 %attend.4.refs_1_ = bf16[1024,256]{1,0:T(8,128)(2,1)} custom-call(s32[1]{0:T(128)} %bitcast.which_ref, bf16[1024,1536]{1,0:T(8,128)(2,1)} %copy-done, bf16[1024,1536]{1,0:T(8,128)(2,1)} %collective-permute-done.10.refs_1_, f32[1024,1]{1,0:T(8,128)} %copy.37.refs_1_.refs_2_, f32[1024,1]{1,0:T(8,128)} %add_rsqrt_fusion.refs_2_.refs_3_, f32[1,6144]{1,0:T(1,128)} %bitcast.29, ...), custom_call_target="tpu_custom_call" | custom-call | flops 15000000512 | bytes 1048576 | tf_op jit(solution)/shard_map/attend/pallas_call | solution.py:217
  288.8 1.5 collective-permute-start.21
  290.3 14.9 %attend.5.refs_2_ = bf16[1024,256]{1,0:T(8,128)(2,1)} custom-call(s32[1]{0:T(128)} %bitcast.which_ref, bf16[1024,1536]{1,0:T(8,128)(2,1)} %copy-done, bf16[1024,1536]{1,0:T(8,128)(2,1)} %collective-permute-done.10.refs_1_, f32[1024,1]{1,0:T(8,128)} %copy.37.refs_1_.refs_2_, f32[1024,1]{1,0:T(8,128)} %add_rsqrt_fusion.refs_2_.refs_3_, f32[1,6144]{1,0:T(1,128)} %bitcast.30, ...), custom_call_target="tpu_custom_call" | custom-call | flops 15000000512 | bytes 1048576 | tf_op jit(solution)/shard_map/attend/pallas_call | solution.py:217
  305.2 6.6 %collective-permute-start.20 = (bf16[1024,256]{1,0:T(8,128)(2,1)}, bf16[1024,256]{1,0:T(8,128)(2,1)}, u32[]{:S(2)}, u32[]{:S(2)}) collective-permute-start(bf16[1024,256]{1,0:T(8,128)(2,1)} %attend.5.refs_2_), channel_id=1, source_target_pairs={{0,1},{1,0},{2,3},{3,2},{4,5},{5,4},{6,7},{7,6},{8,9},{9,8},{10,11... | collective-permute-start | bytes 1572872 | tf_op jit(solution)/shard_map/ppermute | solution.py:54
  311.7 1.5 collective-permute-start.19
  313.2 1.3 collective-permute-start.24
  315.3 7.8 %shard_map.82.refs_4_ = f32[1024,1536]{1,0:T(8,128)} custom-call(s32[2]{0:T(128)} %pad_add_fusion.3.which_ref, bf16[1024,256]{1,0:T(8,128)(2,1)} %attend.3.refs_0_, bf16[1024,256]{1,0:T(8,128)(2,1)} %attend.4.refs_1_, bf16[1024,256]{1,0:T(8,128)(2,1)} %attend.5.refs_2_, bf16[1,768,6144]{2,1,0:T(8,128)(2,1)} %bitcast.31), custom_call_target="tpu_custom_call" | custom-call | flops 15000000512 | bytes 1048576 | tf_op jit(solution)/shard_map/pallas_call | solution.py:268
  323.1 1.8 collective-permute-done.20.refs_2_
  324.9 1.3 collective-permute-start.25
  326.9 1.3 collective-permute-start.18
  328.2 1.3 collective-permute-start.14
  329.5 9.4 %shard_map.83.refs_7_ = f32[1024,1536]{1,0:T(8,128)} custom-call(s32[2]{0:T(128)} %pad_add_fusion.1.which_ref, bf16[1024,256]{1,0:T(8,128)(2,1)} %copy-done.9, bf16[1024,256]{1,0:T(8,128)(2,1)} %copy-done.11, bf16[1024,256]{1,0:T(8,128)(2,1)} %collective-permute-done.20.refs_2_, bf16[4,768,1536]{2,1,0:T(8,128)(2,1)} %all-gather.2.cloned.1.call-done.refs_3_.refs_6_, ...), custom_call_target="tpu_custom_call" | custom-call | flops 15000000512 | bytes 1048576 | tf_op jit(solution)/shard_map/pallas_call | solution.py:268
  338.9 1.3 collective-permute-start.23
  340.2 7.1 %collective-permute-done.25.refs_5_ = bf16[1024,256]{1,0:T(8,128)(2,1)} collective-permute-done((bf16[1024,256]{1,0:T(8,128)(2,1)}, bf16[1024,256]{1,0:T(8,128)(2,1)}, u32[]{:S(2)}, u32[]{:S(2)}) %collective-permute-start.25) | collective-permute-done | bytes 524320 | tf_op jit(solution)/shard_map/ppermute | solution.py:54
  347.4 9.7 %shard_map.84.refs_7_ = f32[1024,1536]{1,0:T(8,128)} custom-call(s32[2]{0:T(128)} %get-tuple-element.65.which_ref, bf16[1024,256]{1,0:T(8,128)(2,1)} %copy-done.6, bf16[1024,256]{1,0:T(8,128)(2,1)} %copy-done.10, bf16[1024,256]{1,0:T(8,128)(2,1)} %copy-done.8, bf16[1024,256]{1,0:T(8,128)(2,1)} %collective-permute-done.24.refs_3_, ...), custom_call_target="tpu_custom_call" | custom-call | flops 15000000512 | bytes 1048576 | tf_op jit(solution)/shard_map/pallas_call | solution.py:268
  357.1 1.4 collective-permute-done.18.refs_3_
  358.5 11.2 %collective-permute-done.14.refs_1_ = bf16[1024,256]{1,0:T(8,128)(2,1)S(1)} collective-permute-done((bf16[1024,256]{1,0:T(8,128)(2,1)S(1)}, bf16[1024,256]{1,0:T(8,128)(2,1)S(1)}, u32[]{:S(2)}, u32[]{:S(2)}) %collective-permute-start.14) | collective-permute-done | bytes 524320 | tf_op jit(solution)/shard_map/ppermute | solution.py:54
  369.7 5.6 %collective-permute-done.23.refs_5_ = bf16[1024,256]{1,0:T(8,128)(2,1)S(1)} collective-permute-done((bf16[1024,256]{1,0:T(8,128)(2,1)S(1)}, bf16[1024,256]{1,0:T(8,128)(2,1)S(1)}, u32[]{:S(2)}, u32[]{:S(2)}) %collective-permute-start.23) | collective-permute-done | bytes 524320 | tf_op jit(solution)/shard_map/ppermute | solution.py:54
  376.1 9.5 %shard_map.85 = bf16[1024,1536]{1,0:T(8,128)(2,1)} custom-call(s32[2]{0:T(128)} %get-tuple-element.66.which_ref, bf16[1024,256]{1,0:T(8,128)(2,1)} %copy-done.7, bf16[1024,256]{1,0:T(8,128)(2,1)} %copy-done.15, bf16[1024,256]{1,0:T(8,128)(2,1)} %copy-done.12, bf16[1024,256]{1,0:T(8,128)(2,1)} %copy-done.14, bf16[1024,256]{1,0:T(8,128)(2,1)} %copy-done.13, ...), custom_call_target="tpu_custom_call" | custom-call | flops 15000000512 | bytes 1048576 | tf_op jit(solution)/shard_map/pallas_call | solution.py:268
  (75 shorter events, 12.4 us)
Async XLA Ops:
  6.5 12.4 %copy-start.1 = (bf16[1024,1536]{1,0:T(8,128)(2,1)S(1)}, bf16[1024,1536]{1,0:T(8,128)(2,1)}, u32[]{:S(2)}) copy-start(bf16[1024,1536]{1,0:T(8,128)(2,1)} %refs_8_.1) | copy-start | bytes 9437188
  6.5 15.9 %copy-start.4 = (s32[1024]{0:T(1024)S(1)}, s32[1024]{0:T(1024)}, u32[]{:S(2)}) copy-start(s32[1024]{0:T(1024)} %param.11) | copy-start | bytes 12292
  6.5 24.9 %copy-start.3 = (s32[1024]{0:T(1024)S(1)}, s32[1024]{0:T(1024)}, u32[]{:S(2)}) copy-start(s32[1024]{0:T(1024)} %param.10) | copy-start | bytes 12292
  6.5 323.0 %all-gather.2.cloned.1.call-start = ((), (), s32[]{:S(2)}) async-start(), calls=%async_computation | async-start | bytes 10616832 | tf_op jit(solution)/shard_map/all_gather | solution.py:347
  9.6 7.0 %collective-permute-start = (f32[2,1024]{1,0:T(2,128)S(1)}, f32[2,1024]{1,0:T(2,128)S(1)}, u32[]{:S(2)}, u32[]{:S(2)}) collective-permute-start(f32[2,1024]{1,0:T(2,128)S(1)} %pad_maximum_fusion), channel_id=1, source_target_pairs={{0,1},{1,2},{2,3},{3,0},{4,5},{5,6},{6,7},{7,4},{8,9},{9,10},{10,1... | collective-permute-start | bytes 24584 | tf_op jit(solution)/shard_map/moments/ppermute | solution.py:325
  12.7 4.6 %collective-permute-start.1 = (f32[2,1024]{1,0:T(2,128)S(1)}, f32[2,1024]{1,0:T(2,128)S(1)}, u32[]{:S(2)}, u32[]{:S(2)}) collective-permute-start(f32[2,1024]{1,0:T(2,128)S(1)} %pad_maximum_fusion), channel_id=1, source_target_pairs={{0,2},{1,3},{2,0},{3,1},{4,6},{5,7},{6,4},{7,5},{8,10},{9,11},{10,... | collective-permute-start | bytes 24584 | tf_op jit(solution)/shard_map/moments/ppermute | solution.py:325
  15.3 3.7 collective-permute-start.2
  19.0 37.5 %collective-permute-start.3 = (bf16[1024,1536]{1,0:T(8,128)(2,1)S(1)}, bf16[1024,1536]{1,0:T(8,128)(2,1)}, u32[]{:S(2)}, u32[]{:S(2)}) collective-permute-start(bf16[1024,1536]{1,0:T(8,128)(2,1)S(1)} %copy-done.1), channel_id=1, source_target_pairs={{1,2},{2,1},{5,6},{6,5},{9,10},{10,9},{13,14},{14,13},{17,18},{18,... | collective-permute-start | bytes 9437192 | tf_op jit(solution)/shard_map/ppermute | solution.py:54
  21.3 68.5 %collective-permute-start.4 = (bf16[1024,1536]{1,0:T(8,128)(2,1)S(1)}, bf16[1024,1536]{1,0:T(8,128)(2,1)}, u32[]{:S(2)}, u32[]{:S(2)}) collective-permute-start(bf16[1024,1536]{1,0:T(8,128)(2,1)S(1)} %copy-done.1), channel_id=1, source_target_pairs={{0,1},{1,0},{2,3},{3,2},{4,5},{5,4},{6,7},{7,6},{8,9},{9,8},{10,11... | collective-permute-start | bytes 9437192 | tf_op jit(solution)/shard_map/ppermute | solution.py:54
  37.7 146.9 %copy-start.2 = (s32[1024]{0:T(1024)}, s32[1024]{0:T(1024)S(1)}, u32[]{:S(2)}) copy-start(s32[1024]{0:T(1024)S(1)} %fusion.3) | copy-start | bytes 12292
  42.9 49.3 %copy-start.5 = (s32[4,3]{1,0:T(4,128)S(1)}, s32[4,3]{1,0:T(4,128)}, u32[]{:S(2)}) copy-start(s32[4,3]{1,0:T(4,128)} %constant.136.clone) | copy-start | bytes 148
  89.9 93.1 %collective-permute-start.5 = (bf16[1024,1536]{1,0:T(8,128)(2,1)}, bf16[1024,1536]{1,0:T(8,128)(2,1)S(1)}, u32[]{:S(2)}, u32[]{:S(2)}) collective-permute-start(bf16[1024,1536]{1,0:T(8,128)(2,1)} %collective-permute-done.4.refs_0_), channel_id=1, source_target_pairs={{1,2},{2,1},{5,6},{6,5},{9,10},{10,9},{13,14},{14,13},{17,18},{18,... | collective-permute-start | bytes 9437192 | tf_op jit(solution)/shard_map/ppermute | solution.py:54
  90.7 92.3 %collective-permute-start.9 = (bf16[1024,1536]{1,0:T(8,128)(2,1)}, bf16[1024,1536]{1,0:T(8,128)(2,1)}, u32[]{:S(2)}, u32[]{:S(2)}) collective-permute-start(bf16[1024,1536]{1,0:T(8,128)(2,1)} %collective-permute-done.3.refs_0_), channel_id=1, source_target_pairs={{1,0},{2,3},{5,4},{6,7},{9,8},{10,11},{13,12},{14,15},{17,16},{18,... | collective-permute-start | bytes 9437192 | tf_op jit(solution)/shard_map/ppermute | solution.py:54
  94.5 28.1 %collective-permute-start.6 = (bf16[96,1536]{1,0:T(8,128)(2,1)S(1)}, bf16[96,1536]{1,0:T(8,128)(2,1)S(1)}, u32[]{:S(2)}, u32[]{:S(2)}) collective-permute-start(bf16[96,1536]{1,0:T(8,128)(2,1)S(1)} %get-tuple-element.59), channel_id=1, source_target_pairs={{0,1},{1,2},{2,3},{3,0},{4,5},{5,6},{6,7},{7,4},{8,9},{9,10},{10,1... | collective-permute-start | bytes 884744 | tf_op jit(solution)/shard_map/ppermute | solution.py:291
  99.4 82.1 %collective-permute-start.7 = (bf16[96,1536]{1,0:T(8,128)(2,1)S(1)}, bf16[96,1536]{1,0:T(8,128)(2,1)S(1)}, u32[]{:S(2)}, u32[]{:S(2)}) collective-permute-start(bf16[96,1536]{1,0:T(8,128)(2,1)S(1)} %get-tuple-element.58), channel_id=1, source_target_pairs={{0,2},{1,3},{2,0},{3,1},{4,6},{5,7},{6,4},{7,5},{8,10},{9,11},{10,... | collective-permute-start | bytes 884744 | tf_op jit(solution)/shard_map/ppermute | solution.py:291
  100.2 82.0 %collective-permute-start.8 = (bf16[96,1536]{1,0:T(8,128)(2,1)S(1)}, bf16[96,1536]{1,0:T(8,128)(2,1)S(1)}, u32[]{:S(2)}, u32[]{:S(2)}) collective-permute-start(bf16[96,1536]{1,0:T(8,128)(2,1)S(1)} %get-tuple-element.57), channel_id=1, source_target_pairs={{0,3},{1,0},{2,1},{3,2},{4,7},{5,4},{6,5},{7,6},{8,11},{9,8},{10,9... | collective-permute-start | bytes 884744 | tf_op jit(solution)/shard_map/ppermute | solution.py:291
  183.0 24.3 %copy-start = (bf16[1024,1536]{1,0:T(8,128)(2,1)}, bf16[1024,1536]{1,0:T(8,128)(2,1)S(1)}, u32[]{:S(2)}) copy-start(bf16[1024,1536]{1,0:T(8,128)(2,1)S(1)} %collective-permute-done.5.refs_0_) | copy-start | bytes 9437188
  183.0 69.2 %collective-permute-start.10 = (bf16[1024,1536]{1,0:T(8,128)(2,1)S(1)}, bf16[1024,1536]{1,0:T(8,128)(2,1)}, u32[]{:S(2)}, u32[]{:S(2)}) collective-permute-start(bf16[1024,1536]{1,0:T(8,128)(2,1)S(1)} %collective-permute-done.5.refs_0_), channel_id=1, source_target_pairs={{1,0},{2,3},{5,4},{6,7},{9,8},{10,11},{13,12},{14,15},{17,16},{18,... | collective-permute-start | bytes 9437192 | tf_op jit(solution)/shard_map/ppermute | solution.py:54
  267.1 21.0 %collective-permute-start.11 = (bf16[1024,256]{1,0:T(8,128)(2,1)}, bf16[1024,256]{1,0:T(8,128)(2,1)S(1)}, u32[]{:S(2)}, u32[]{:S(2)}) collective-permute-start(bf16[1024,256]{1,0:T(8,128)(2,1)} %attend.3.refs_0_), channel_id=1, source_target_pairs={{1,2},{2,1},{5,6},{6,5},{9,10},{10,9},{13,14},{14,13},{17,18},{18,... | collective-permute-start | bytes 1572872 | tf_op jit(solution)/shard_map/ppermute | solution.py:54
  267.8 20.3 %collective-permute-start.12 = (bf16[1024,256]{1,0:T(8,128)(2,1)}, bf16[1024,256]{1,0:T(8,128)(2,1)S(1)}, u32[]{:S(2)}, u32[]{:S(2)}) collective-permute-start(bf16[1024,256]{1,0:T(8,128)(2,1)} %attend.3.refs_0_), channel_id=1, source_target_pairs={{0,1},{1,0},{2,3},{3,2},{4,5},{5,4},{6,7},{7,6},{8,9},{9,8},{10,11... | collective-permute-start | bytes 1572872 | tf_op jit(solution)/shard_map/ppermute | solution.py:54
  287.3 24.4 %collective-permute-start.16 = (bf16[1024,256]{1,0:T(8,128)(2,1)}, bf16[1024,256]{1,0:T(8,128)(2,1)S(1)}, u32[]{:S(2)}, u32[]{:S(2)}) collective-permute-start(bf16[1024,256]{1,0:T(8,128)(2,1)} %attend.4.refs_1_), channel_id=1, source_target_pairs={{0,1},{1,0},{2,3},{3,2},{4,5},{5,4},{6,7},{7,6},{8,9},{9,8},{10,11... | collective-permute-start | bytes 1572872 | tf_op jit(solution)/shard_map/ppermute | solution.py:54
  287.3 25.9 %collective-permute-start.15 = (bf16[1024,256]{1,0:T(8,128)(2,1)}, bf16[1024,256]{1,0:T(8,128)(2,1)S(1)}, u32[]{:S(2)}, u32[]{:S(2)}) collective-permute-start(bf16[1024,256]{1,0:T(8,128)(2,1)} %attend.4.refs_1_), channel_id=1, source_target_pairs={{1,2},{2,1},{5,6},{6,5},{9,10},{10,9},{13,14},{14,13},{17,18},{18,... | collective-permute-start | bytes 1572872 | tf_op jit(solution)/shard_map/ppermute | solution.py:54
  288.0 17.1 %copy-start.6 = (bf16[1024,256]{1,0:T(8,128)(2,1)}, bf16[1024,256]{1,0:T(8,128)(2,1)S(1)}, u32[]{:S(2)}) copy-start(bf16[1024,256]{1,0:T(8,128)(2,1)S(1)} %collective-permute-done.11.refs_0_) | copy-start | bytes 1572868
  288.1 17.1 %copy-start.9 = (bf16[1024,256]{1,0:T(8,128)(2,1)}, bf16[1024,256]{1,0:T(8,128)(2,1)S(1)}, u32[]{:S(2)}) copy-start(bf16[1024,256]{1,0:T(8,128)(2,1)S(1)} %collective-permute-done.12.refs_0_) | copy-start | bytes 1572868
  288.1 26.4 %collective-permute-start.13 = (bf16[1024,256]{1,0:T(8,128)(2,1)S(1)}, bf16[1024,256]{1,0:T(8,128)(2,1)S(1)}, u32[]{:S(2)}, u32[]{:S(2)}) collective-permute-start(bf16[1024,256]{1,0:T(8,128)(2,1)S(1)} %collective-permute-done.12.refs_0_), channel_id=1, source_target_pairs={{1,2},{2,1},{5,6},{6,5},{9,10},{10,9},{13,14},{14,13},{17,18},{18,... | collective-permute-start | bytes 1572872 | tf_op jit(solution)/shard_map/ppermute | solution.py:54
  288.8 26.5 %collective-permute-start.21 = (bf16[1024,256]{1,0:T(8,128)(2,1)S(1)}, bf16[1024,256]{1,0:T(8,128)(2,1)S(1)}, u32[]{:S(2)}, u32[]{:S(2)}) collective-permute-start(bf16[1024,256]{1,0:T(8,128)(2,1)S(1)} %collective-permute-done.11.refs_0_), channel_id=1, source_target_pairs={{1,0},{2,3},{5,4},{6,7},{9,8},{10,11},{13,12},{14,15},{17,16},{18,... | collective-permute-start | bytes 1572872 | tf_op jit(solution)/shard_map/ppermute | solution.py:54
  305.2 19.7 %collective-permute-start.20 = (bf16[1024,256]{1,0:T(8,128)(2,1)}, bf16[1024,256]{1,0:T(8,128)(2,1)}, u32[]{:S(2)}, u32[]{:S(2)}) collective-permute-start(bf16[1024,256]{1,0:T(8,128)(2,1)} %attend.5.refs_2_), channel_id=1, source_target_pairs={{0,1},{1,0},{2,3},{3,2},{4,5},{5,4},{6,7},{7,6},{8,9},{9,8},{10,11... | collective-permute-start | bytes 1572872 | tf_op jit(solution)/shard_map/ppermute | solution.py:54
  311.7 11.3 %copy-start.11 = (bf16[1024,256]{1,0:T(8,128)(2,1)}, bf16[1024,256]{1,0:T(8,128)(2,1)S(1)}, u32[]{:S(2)}) copy-start(bf16[1024,256]{1,0:T(8,128)(2,1)S(1)} %collective-permute-done.16.refs_1_) | copy-start | bytes 1572868
  311.7 13.2 %collective-permute-start.19 = (bf16[1024,256]{1,0:T(8,128)(2,1)}, bf16[1024,256]{1,0:T(8,128)(2,1)}, u32[]{:S(2)}, u32[]{:S(2)}) collective-permute-start(bf16[1024,256]{1,0:T(8,128)(2,1)} %attend.5.refs_2_), channel_id=1, source_target_pairs={{1,2},{2,1},{5,6},{6,5},{9,10},{10,9},{13,14},{14,13},{17,18},{18,... | collective-permute-start | bytes 1572872 | tf_op jit(solution)/shard_map/ppermute | solution.py:54
  313.2 9.8 %copy-start.8 = (bf16[1024,256]{1,0:T(8,128)(2,1)}, bf16[1024,256]{1,0:T(8,128)(2,1)S(1)}, u32[]{:S(2)}) copy-start(bf16[1024,256]{1,0:T(8,128)(2,1)S(1)} %collective-permute-done.15.refs_2_) | copy-start | bytes 1572868
  313.2 27.0 %collective-permute-start.24 = (bf16[1024,256]{1,0:T(8,128)(2,1)S(1)}, bf16[1024,256]{1,0:T(8,128)(2,1)}, u32[]{:S(2)}, u32[]{:S(2)}) collective-permute-start(bf16[1024,256]{1,0:T(8,128)(2,1)S(1)} %collective-permute-done.15.refs_2_), channel_id=1, source_target_pairs={{1,0},{2,3},{5,4},{6,7},{9,8},{10,11},{13,12},{14,15},{17,16},{18,... | collective-permute-start | bytes 1572872 | tf_op jit(solution)/shard_map/ppermute | solution.py:54
  314.5 13.7 %copy-start.7 = (bf16[1024,256]{1,0:T(8,128)(2,1)}, bf16[1024,256]{1,0:T(8,128)(2,1)S(1)}, u32[]{:S(2)}) copy-start(bf16[1024,256]{1,0:T(8,128)(2,1)S(1)} %collective-permute-done.13.refs_0_) | copy-start | bytes 1572868
  314.5 12.3 %collective-permute-start.17 = (bf16[1024,256]{1,0:T(8,128)(2,1)S(1)}, bf16[1024,256]{1,0:T(8,128)(2,1)S(1)}, u32[]{:S(2)}, u32[]{:S(2)}) collective-permute-start(bf16[1024,256]{1,0:T(8,128)(2,1)S(1)} %collective-permute-done.16.refs_1_), channel_id=1, source_target_pairs={{1,2},{2,1},{5,6},{6,5},{9,10},{10,9},{13,14},{14,13},{17,18},{18,... | collective-permute-start | bytes 1572872 | tf_op jit(solution)/shard_map/ppermute | solution.py:54
  315.2 7.8 %copy-start.10 = (bf16[1024,256]{1,0:T(8,128)(2,1)}, bf16[1024,256]{1,0:T(8,128)(2,1)S(1)}, u32[]{:S(2)}) copy-start(bf16[1024,256]{1,0:T(8,128)(2,1)S(1)} %collective-permute-done.21.refs_1_) | copy-start | bytes 1572868
  324.9 22.5 %collective-permute-start.25 = (bf16[1024,256]{1,0:T(8,128)(2,1)}, bf16[1024,256]{1,0:T(8,128)(2,1)}, u32[]{:S(2)}, u32[]{:S(2)}) collective-permute-start(bf16[1024,256]{1,0:T(8,128)(2,1)} %collective-permute-done.19.refs_4_), channel_id=1, source_target_pairs={{1,0},{2,3},{5,4},{6,7},{9,8},{10,11},{13,12},{14,15},{17,16},{18,... | collective-permute-start | bytes 1572872 | tf_op jit(solution)/shard_map/ppermute | solution.py:54
  326.2 12.7 %collective-permute-start.22 = (bf16[1024,256]{1,0:T(8,128)(2,1)}, bf16[1024,256]{1,0:T(8,128)(2,1)S(1)}, u32[]{:S(2)}, u32[]{:S(2)}) collective-permute-start(bf16[1024,256]{1,0:T(8,128)(2,1)} %collective-permute-done.20.refs_2_), channel_id=1, source_target_pairs={{1,2},{2,1},{5,6},{6,5},{9,10},{10,9},{13,14},{14,13},{17,18},{18,... | collective-permute-start | bytes 1572872 | tf_op jit(solution)/shard_map/ppermute | solution.py:54
  326.9 12.0 %copy-start.12 = (bf16[1024,256]{1,0:T(8,128)(2,1)}, bf16[1024,256]{1,0:T(8,128)(2,1)S(1)}, u32[]{:S(2)}) copy-start(bf16[1024,256]{1,0:T(8,128)(2,1)S(1)} %collective-permute-done.17.refs_2_) | copy-start | bytes 1572868
  326.9 31.6 %collective-permute-start.18 = (bf16[1024,256]{1,0:T(8,128)(2,1)S(1)}, bf16[1024,256]{1,0:T(8,128)(2,1)S(1)}, u32[]{:S(2)}, u32[]{:S(2)}) collective-permute-start(bf16[1024,256]{1,0:T(8,128)(2,1)S(1)} %collective-permute-done.17.refs_2_), channel_id=1, source_target_pairs={{1,0},{2,3},{5,4},{6,7},{9,8},{10,11},{13,12},{14,15},{17,16},{18,... | collective-permute-start | bytes 1572872 | tf_op jit(solution)/shard_map/ppermute | solution.py:54
  328.2 41.5 %collective-permute-start.14 = (bf16[1024,256]{1,0:T(8,128)(2,1)S(1)}, bf16[1024,256]{1,0:T(8,128)(2,1)S(1)}, u32[]{:S(2)}, u32[]{:S(2)}) collective-permute-start(bf16[1024,256]{1,0:T(8,128)(2,1)S(1)} %collective-permute-done.13.refs_0_), channel_id=1, source_target_pairs={{1,0},{2,3},{5,4},{6,7},{9,8},{10,11},{13,12},{14,15},{17,16},{18,... | collective-permute-start | bytes 1572872 | tf_op jit(solution)/shard_map/ppermute | solution.py:54
  338.9 18.2 %copy-start.13 = (bf16[1024,256]{1,0:T(8,128)(2,1)}, bf16[1024,256]{1,0:T(8,128)(2,1)S(1)}, u32[]{:S(2)}) copy-start(bf16[1024,256]{1,0:T(8,128)(2,1)S(1)} %collective-permute-done.22.refs_4_) | copy-start | bytes 1572868
  338.9 36.4 %collective-permute-start.23 = (bf16[1024,256]{1,0:T(8,128)(2,1)S(1)}, bf16[1024,256]{1,0:T(8,128)(2,1)S(1)}, u32[]{:S(2)}, u32[]{:S(2)}) collective-permute-start(bf16[1024,256]{1,0:T(8,128)(2,1)S(1)} %collective-permute-done.22.refs_4_), channel_id=1, source_target_pairs={{1,0},{2,3},{5,4},{6,7},{9,8},{10,11},{13,12},{14,15},{17,16},{18,... | collective-permute-start | bytes 1572872 | tf_op jit(solution)/shard_map/ppermute | solution.py:54
  358.5 16.9 %copy-start.14 = (bf16[1024,256]{1,0:T(8,128)(2,1)}, bf16[1024,256]{1,0:T(8,128)(2,1)S(1)}, u32[]{:S(2)}) copy-start(bf16[1024,256]{1,0:T(8,128)(2,1)S(1)} %collective-permute-done.18.refs_3_) | copy-start | bytes 1572868
  369.7 5.6 %copy-start.15 = (bf16[1024,256]{1,0:T(8,128)(2,1)}, bf16[1024,256]{1,0:T(8,128)(2,1)S(1)}, u32[]{:S(2)}) copy-start(bf16[1024,256]{1,0:T(8,128)(2,1)S(1)} %collective-permute-done.14.refs_1_) | copy-start | bytes 1572868
  375.4 0.8 copy-start.16
Sparse Core Ops, SparseCore 0:
  183.2 62.2 all-gather.1
where the time goes:
time: 393 us
  waiting for transfers between devices  166 us (42%)
  Pallas kernels  129 us (33%)
  starting transfers between devices  46.8 us (12%)
  local copies, waits for them, and re-layouts  18.8 us (5%)
  between operations  13.9 us (4%)
  blocking collectives  9.07 us (2%)
  other arithmetic  8.97 us (2%)
    ppermute x20, waiting for transfers between devices, step(): self.got[s, kind] = lax.ppermute(source, self.axis, self.steps[s, kind])  105 us
    ppermute x3, waiting for transfers between devices, exchange_out_weight(): lax.ppermute(columns((place + d) % n), 'mp', [(i, (i + d) % n) for i in r...  58.2 us
    pallas_call x3, Pallas kernels, project(): pl.pallas_call(kernel, grid_spec=pltpu.PrefetchScalarGridSpec(num_scalar_...  48 us
    pallas_call x3, Pallas kernels, attend(): pl.pallas_call(kernel, grid_spec=pltpu.PrefetchScalarGridSpec(num_scalar_...  44.5 us
    pallas_call x4, Pallas kernels, project_out(): pl.pallas_call(kernel, grid_spec=pltpu.PrefetchScalarGridSpec(num_scalar_...  36.4 us
    ppermute x20, starting transfers between devices, step(): self.got[s, kind] = lax.ppermute(source, self.axis, self.steps[s, kind])  31.2 us
    all_gather x1, blocking collectives, shards(): segment = lax.all_gather(segment_ids, 'dp', tiled=True)[dest_pos]  9.07 us
    ppermute x3, starting transfers between devices, exchange_out_weight(): lax.ppermute(columns((place + d) % n), 'mp', [(i, (i + d) % n) for i in r...  8.57 us
  transfers between devices with their start and end apart: 27, of which 10 were waited for; matrix products, arithmetic and copies ran while one was open for 6% of the time, Pallas kernels for 30%

commit v1 on v0

--- a/solution.py
+++ b/solution.py
@@ -236,7 +236,7 @@
     rows = pieces[0][0].shape[0]
     _, depth, _ = weight.shape
     width = which[1]
-    high = pick(rows, 256)
+    high = pick(rows, 512)
     flat = [array for piece in pieces for array in piece]
 
     def kernel(which_ref, *refs):
@@ -323,10 +323,6 @@
         sums = moments
         for d in range(1, n):
             sums = sums + lax.ppermute(moments, "mp", [(i, (i + d) % n) for i in range(n)])
-        average = sums[0] / features
-        variance = sums[1] / features - average * average
-        inverse = lax.rsqrt(variance + EPS)
-        norm = (average[:, None], inverse[:, None], norm_gain[None, :])
 
     sources = origins("mp", n)
 
@@ -335,16 +331,22 @@
             return project(parts, norm, qkv_weight, origin, acc)
 
     line = Relay(tokens, "mp", n)
-    line.step(1, sums)
-    projected = step_project([tokens], place, None)
-    pieces = out_weight
+    line.step(1)
+    projected = None
     for s in range(2, n):
         there = [line.got[key] for key in line.steps if key[0] == s - 1]
-        pieces = line.step(s, projected, block, pieces, *there)[2]
+        ready = [] if projected is None else [projected]
+        _, sums, *ready = line.step(s, block, sums, *ready, *there)[: 2 + len(ready)]
         if s == 2:
-            pieces = stack(exchange_out_weight(pieces, n, groups))
-        elif s == 3:
-            out_columns = lax.all_gather(pieces, "dp", axis=1, tiled=True)
+            average = sums[0] / features
+            variance = sums[1] / features - average * average
+            inverse = lax.rsqrt(variance + EPS)
+            norm = (average[:, None], inverse[:, None], norm_gain[None, :])
+            projected = step_project([tokens], place, None)
+            pieces = lax.optimization_barrier((out_weight, projected))[0]
+            received = exchange_out_weight(pieces, n, groups)
+        else:
+            projected = ready[0]
         projected = step_project(line.arrived(s - 2), sources[s - 2], projected)
     last = line.arrived(n - 2)
 
@@ -365,6 +367,9 @@
         lines.append(Relay(context, "mp", n))
         lines[-1].step(1)
 
+    pieces = lax.optimization_barrier((*[array for _, array in received], contexts[0]))
+    pieces = stack([(origin, array) for (origin, _), array in zip(received, pieces)])
+    out_columns = lax.all_gather(pieces, "dp", axis=1, tiled=True)
     zero = jnp.zeros((), jnp.int32)
 
     def step_out(k, acc, residual):

time: 393 us -> 381 us (0.969)
  Pallas kernels: 129 us -> 125 us
    ppermute x3, waiting for transfers between devices: 58.2 us -> 0.01 us  [exchange_out_weight(): lax.ppermute(columns((place + d) % n), 'mp', [(i, (i + d) % n) for i in r...]
    ppermute x3, waiting for transfers between devices: 2.3 us -> 46.9 us  [shards(): lax.ppermute(moments, 'mp', [(i, (i + d) % n) for i in range(n)])]
    ppermute x20, waiting for transfers between devices: 105 us -> 117 us  [step(): self.got[s, kind] = lax.ppermute(source, self.axis, self.steps[s, kind])]
    dynamic_update_slice x4, local copies, waits for them, and re-layouts: 4.13 us -> 0.11 us  [stack(): lax.dynamic_update_slice_in_dim(pieces, array[None], origin, axis=0)]
  transfers between devices with their start and end apart: 27 -> 27, of which waited for: 10 -> 8; matrix products, arithmetic and copies ran while one was open for 6% -> 6% of each run, Pallas kernels for 30% -> 31%
where the time goes in v1:
time: 381 us; the launch traced here: 380 us
  waiting for transfers between devices  164 us (43%)
  Pallas kernels  125 us (33%)
  starting transfers between devices  43.8 us (11%)
  local copies, waits for them, and re-layouts  14.9 us (4%)
  between operations  13.9 us (4%)
  blocking collectives  9.07 us (2%)
  other arithmetic  8.74 us (2%)
    ppermute x20, waiting for transfers between devices, step(): self.got[s, kind] = lax.ppermute(source, self.axis, self.steps[s, kind])  117 us
    pallas_call x3, Pallas kernels, project(): pl.pallas_call(kernel, grid_spec=pltpu.PrefetchScalarGridSpec(num_scalar_...  47.2 us
    ppermute x3, waiting for transfers between devices, shards(): lax.ppermute(moments, 'mp', [(i, (i + d) % n) for i in range(n)])  46.9 us
    pallas_call x3, Pallas kernels, attend(): pl.pallas_call(kernel, grid_spec=pltpu.PrefetchScalarGridSpec(num_scalar_...  45.2 us
    pallas_call x4, Pallas kernels, project_out(): pl.pallas_call(kernel, grid_spec=pltpu.PrefetchScalarGridSpec(num_scalar_...  32.6 us
    ppermute x20, starting transfers between devices, step(): self.got[s, kind] = lax.ppermute(source, self.axis, self.steps[s, kind])  31.7 us
    all_gather x1, blocking collectives, shards(): segment = lax.all_gather(segment_ids, 'dp', tiled=True)[dest_pos]  9.07 us
    ppermute x3, starting transfers between devices, exchange_out_weight(): lax.ppermute(columns((place + d) % n), 'mp', [(i, (i + d) % n) for i in r...  7.86 us
  transfers between devices with their start and end apart: 27, of which 8 were waited for; matrix products, arithmetic and copies ran while one was open for 6% of the time, Pallas kernels for 31%

profile of v1, /device:TPU:0, one launch (start us, length us, event | category | flops | bytes accessed | tf_op | source)
XLA Modules:
  0.0 379.9 jit_solution(10817664587650020577)
XLA Ops:
  6.5 2.4 collective-permute-start
  9.0 4.3 %collective-permute-start.1 = (bf16[1024,1536]{1,0:T(8,128)(2,1)}, bf16[1024,1536]{1,0:T(8,128)(2,1)}, u32[]{:S(2)}, u32[]{:S(2)}) collective-permute-start(bf16[1024,1536]{1,0:T(8,128)(2,1)} %refs_8_.1), channel_id=1, source_target_pairs={{0,1},{1,0},{2,3},{3,2},{4,5},{5,4},{6,7},{7,6},{8,9},{9,8},{10,11... | collective-permute-start | bytes 9437192 | tf_op jit(solution)/shard_map/ppermute | solution.py:54
  13.3 2.9 convert_reduce_fusion
  16.3 1.9 collective-permute-start.3
  18.2 2.4 collective-permute-start.4
  20.5 9.1 %all_gather.6 = s32[8192]{0:T(1024)S(1)} all-gather(s32[1024]{0:T(1024)S(1)} %copy-done.5), channel_id=1, replica_groups=mesh['dp'=8,'mp'=4] {'dp'}, dimensions={0}, use_global_device_ids=true | all-gather | bytes 36864 | tf_op jit(solution)/shard_map/all_gather | solution.py:314
  29.6 6.1 %gather_fusion = s32[1024]{0:T(1024)S(1)} fusion(s32[8192]{0:T(1024)S(1)} %all_gather.6, s32[1024]{0:T(1024)S(1)} %fusion.4), kind=kCustom, calls=%fused_computation | custom fusion | bytes 12288 | tf_op jit(solution)/shard_map/gather | solution.py:314
  35.8 46.9 %collective-permute-done.2 = f32[2,1024]{1,0:T(2,128)S(1)} collective-permute-done((f32[2,1024]{1,0:T(2,128)S(1)}, f32[2,1024]{1,0:T(2,128)S(1)}, u32[]{:S(2)}, u32[]{:S(2)}) %collective-permute-start.2) | collective-permute-done | bytes 8224 | tf_op jit(solution)/shard_map/moments/ppermute | solution.py:325
  82.8 0.9 collective-permute-start.5
  83.6 1.3 collective-permute-start.6
  85.6 1.0 copy.35
  86.6 1.0 copy.36
  87.6 1.0 copy.38.refs_1_.refs_2_
  88.7 2.1 add_rsqrt_fusion.refs_2_.refs_3_
  90.7 13.6 %project.3.refs_5_ = f32[3,1024,768]{2,1,0:T(8,128)} custom-call(s32[1]{0:T(128)} %bitcast.7.which_ref, bf16[1024,1536]{1,0:T(8,128)(2,1)} %refs_8_.1, f32[1024,1]{1,0:T(8,128)} %copy.38.refs_1_.refs_2_, f32[1024,1]{1,0:T(8,128)} %add_rsqrt_fusion.refs_2_.refs_3_, f32[1,6144]{1,0:T(1,128)} %bitcast.25, bf16[3,6144,768]{2,1,0:T(8,128)(2,1)} %refs_7_.5), custom_call_target="tpu_custom_call" | custom-call | flops 7247757312 | bytes 25952256 | tf_op jit(solution)/shard_map/project/pallas_call | solution.py:117
  104.3 16.4 %project.4.refs_6_ = f32[3,1024,768]{2,1,0:T(8,128)} custom-call(s32[1]{0:T(128)} %bitcast.3.which_ref, bf16[1024,1536]{1,0:T(8,128)(2,1)} %collective-permute-done.1.refs_0_, f32[1024,1]{1,0:T(8,128)} %copy.38.refs_1_.refs_2_, f32[1024,1]{1,0:T(8,128)} %add_rsqrt_fusion.refs_2_.refs_3_, f32[1,6144]{1,0:T(1,128)} %bitcast.26, ...), custom_call_target="tpu_custom_call", output_to_operand_aliasing={{}: (6, {})} | custom-call | flops 7247757312 | bytes 25952256 | tf_op jit(solution)/shard_map/project/pallas_call | solution.py:117
  120.7 34.1 %collective-permute-done.6.refs_1_ = bf16[1024,1536]{1,0:T(8,128)(2,1)} collective-permute-done((bf16[1024,1536]{1,0:T(8,128)(2,1)}, bf16[1024,1536]{1,0:T(8,128)(2,1)}, u32[]{:S(2)}, u32[]{:S(2)}) %collective-permute-start.6) | collective-permute-done | bytes 3145760 | tf_op jit(solution)/shard_map/ppermute | solution.py:54
  154.7 1.3 collective-permute-start.7
  156.1 1.0 copy.41.refs_12_
  157.2 2.0 fusion.7
  159.1 4.3 %collective-permute-start.20 = (bf16[96,1536]{1,0:T(8,128)(2,1)S(1)}, bf16[96,1536]{1,0:T(8,128)(2,1)S(1)}, u32[]{:S(2)}, u32[]{:S(2)}) collective-permute-start(bf16[96,1536]{1,0:T(8,128)(2,1)S(1)} %get-tuple-element.69), channel_id=1, source_target_pairs={{0,1},{1,2},{2,3},{3,0},{4,5},{5,6},{6,7},{7,4},{8,9},{9,10},{10,1... | collective-permute-start | bytes 884744 | tf_op jit(solution)/shard_map/ppermute | solution.py:291
  164.2 2.8 collective-permute-start.22
  167.0 17.2 %project.5.refs_8_.refs_9_.refs_10_ = f32[3,1024,768]{2,1,0:T(8,128)} custom-call(s32[1]{0:T(128)} %bitcast.8.which_ref, bf16[1024,1536]{1,0:T(8,128)(2,1)} %collective-permute-done.refs_0_, bf16[1024,1536]{1,0:T(8,128)(2,1)} %collective-permute-done.6.refs_1_, f32[1024,1]{1,0:T(8,128)} %copy.38.refs_1_.refs_2_, ...), custom_call_target="tpu_custom_call", output_to_operand_aliasing={{}: (7, {})} | custom-call | flops 7247757312 | bytes 25952256 | tf_op jit(solution)/shard_map/project/pallas_call | solution.py:117
  184.2 55.6 %collective-permute-done.7.refs_1_ = bf16[1024,1536]{1,0:T(8,128)(2,1)} collective-permute-done((bf16[1024,1536]{1,0:T(8,128)(2,1)S(1)}, bf16[1024,1536]{1,0:T(8,128)(2,1)}, u32[]{:S(2)}, u32[]{:S(2)}) %collective-permute-start.7) | collective-permute-done | bytes 3145760 | tf_op jit(solution)/shard_map/ppermute | solution.py:54
  239.9 14.9 %attend.3.refs_0_ = bf16[1024,256]{1,0:T(8,128)(2,1)} custom-call(s32[1]{0:T(128)} %bitcast.which_ref, bf16[1024,1536]{1,0:T(8,128)(2,1)} %copy-done, bf16[1024,1536]{1,0:T(8,128)(2,1)} %collective-permute-done.7.refs_1_, f32[1024,1]{1,0:T(8,128)} %copy.38.refs_1_.refs_2_, f32[1024,1]{1,0:T(8,128)} %add_rsqrt_fusion.refs_2_.refs_3_, f32[1,6144]{1,0:T(1,128)} %bitcast.28, ...), custom_call_target="tpu_custom_call" | custom-call | flops 15000000512 | bytes 1048576 | tf_op jit(solution)/shard_map/attend/pallas_call | solution.py:217
  255.0 1.0 copy-done.1
  256.7 1.3 pad_add_fusion.1.which_ref
  257.9 1.8 pad_add_fusion
  260.5 2.0 collective-permute-start.9
  262.5 15.5 %attend.4.refs_1_ = bf16[1024,256]{1,0:T(8,128)(2,1)} custom-call(s32[1]{0:T(128)} %bitcast.which_ref, bf16[1024,1536]{1,0:T(8,128)(2,1)} %copy-done, bf16[1024,1536]{1,0:T(8,128)(2,1)} %collective-permute-done.7.refs_1_, f32[1024,1]{1,0:T(8,128)} %copy.38.refs_1_.refs_2_, f32[1024,1]{1,0:T(8,128)} %add_rsqrt_fusion.refs_2_.refs_3_, f32[1,6144]{1,0:T(1,128)} %bitcast.29, ...), custom_call_target="tpu_custom_call" | custom-call | flops 15000000512 | bytes 1048576 | tf_op jit(solution)/shard_map/attend/pallas_call | solution.py:217
  279.8 1.5 collective-permute-start.18
  281.3 14.8 %attend.5.refs_2_ = bf16[1024,256]{1,0:T(8,128)(2,1)} custom-call(s32[1]{0:T(128)} %bitcast.which_ref, bf16[1024,1536]{1,0:T(8,128)(2,1)} %copy-done, bf16[1024,1536]{1,0:T(8,128)(2,1)} %collective-permute-done.7.refs_1_, f32[1024,1]{1,0:T(8,128)} %copy.38.refs_1_.refs_2_, f32[1024,1]{1,0:T(8,128)} %add_rsqrt_fusion.refs_2_.refs_3_, f32[1,6144]{1,0:T(1,128)} %bitcast.30, ...), custom_call_target="tpu_custom_call" | custom-call | flops 15000000512 | bytes 1048576 | tf_op jit(solution)/shard_map/attend/pallas_call | solution.py:217
  296.1 6.3 %collective-permute-start.17 = (bf16[1024,256]{1,0:T(8,128)(2,1)}, bf16[1024,256]{1,0:T(8,128)(2,1)}, u32[]{:S(2)}, u32[]{:S(2)}) collective-permute-start(bf16[1024,256]{1,0:T(8,128)(2,1)} %attend.5.refs_2_), channel_id=1, source_target_pairs={{0,1},{1,0},{2,3},{3,2},{4,5},{5,4},{6,7},{7,6},{8,9},{9,8},{10,11... | collective-permute-start | bytes 1572872 | tf_op jit(solution)/shard_map/ppermute | solution.py:54
  302.4 1.5 collective-permute-start.16
  303.9 1.3 collective-permute-start.24
  305.9 7.3 %shard_map.82.refs_4_ = f32[1024,1536]{1,0:T(8,128)} custom-call(s32[2]{0:T(128)} %pad_add_fusion.3.which_ref, bf16[1024,256]{1,0:T(8,128)(2,1)} %attend.3.refs_0_, bf16[1024,256]{1,0:T(8,128)(2,1)} %attend.4.refs_1_, bf16[1024,256]{1,0:T(8,128)(2,1)} %attend.5.refs_2_, bf16[1,768,6144]{2,1,0:T(8,128)(2,1)} %bitcast.31), custom_call_target="tpu_custom_call" | custom-call | flops 15000000512 | bytes 1048576 | tf_op jit(solution)/shard_map/pallas_call | solution.py:268
  313.3 1.7 collective-permute-done.17.refs_2_
  314.9 1.3 collective-permute-start.25
  316.9 1.3 collective-permute-start.15
  318.3 1.3 collective-permute-start.11
  319.6 8.2 %shard_map.83.refs_7_ = f32[1024,1536]{1,0:T(8,128)} custom-call(s32[2]{0:T(128)} %pad_add_fusion.1.which_ref, bf16[1024,256]{1,0:T(8,128)(2,1)} %copy-done.10, bf16[1024,256]{1,0:T(8,128)(2,1)} %copy-done.12, bf16[1024,256]{1,0:T(8,128)(2,1)} %collective-permute-done.17.refs_2_, bf16[4,768,1536]{2,1,0:T(8,128)(2,1)} %all-gather.2.cloned.1.call-done.refs_3_.refs_6_, ...), custom_call_target="tpu_custom_call" | custom-call | flops 15000000512 | bytes 1048576 | tf_op jit(solution)/shard_map/pallas_call | solution.py:268
  327.8 1.3 collective-permute-start.23
  329.1 8.3 %collective-permute-done.25.refs_5_ = bf16[1024,256]{1,0:T(8,128)(2,1)} collective-permute-done((bf16[1024,256]{1,0:T(8,128)(2,1)}, bf16[1024,256]{1,0:T(8,128)(2,1)}, u32[]{:S(2)}, u32[]{:S(2)}) %collective-permute-start.25) | collective-permute-done | bytes 524320 | tf_op jit(solution)/shard_map/ppermute | solution.py:54
  337.4 8.5 %shard_map.84.refs_7_ = f32[1024,1536]{1,0:T(8,128)} custom-call(s32[2]{0:T(128)} %get-tuple-element.76.which_ref, bf16[1024,256]{1,0:T(8,128)(2,1)} %copy-done.7, bf16[1024,256]{1,0:T(8,128)(2,1)} %copy-done.11, bf16[1024,256]{1,0:T(8,128)(2,1)} %copy-done.9, bf16[1024,256]{1,0:T(8,128)(2,1)} %collective-permute-done.24.refs_3_, ...), custom_call_target="tpu_custom_call" | custom-call | flops 15000000512 | bytes 1048576 | tf_op jit(solution)/shard_map/pallas_call | solution.py:268
  345.9 2.6 collective-permute-done.15.refs_3_
  348.5 9.4 %collective-permute-done.11.refs_1_ = bf16[1024,256]{1,0:T(8,128)(2,1)S(1)} collective-permute-done((bf16[1024,256]{1,0:T(8,128)(2,1)S(1)}, bf16[1024,256]{1,0:T(8,128)(2,1)S(1)}, u32[]{:S(2)}, u32[]{:S(2)}) %collective-permute-start.11) | collective-permute-done | bytes 524320 | tf_op jit(solution)/shard_map/ppermute | solution.py:54
  358.0 5.6 %collective-permute-done.23.refs_5_ = bf16[1024,256]{1,0:T(8,128)(2,1)S(1)} collective-permute-done((bf16[1024,256]{1,0:T(8,128)(2,1)S(1)}, bf16[1024,256]{1,0:T(8,128)(2,1)S(1)}, u32[]{:S(2)}, u32[]{:S(2)}) %collective-permute-start.23) | collective-permute-done | bytes 524320 | tf_op jit(solution)/shard_map/ppermute | solution.py:54
  364.4 8.6 %shard_map.85 = bf16[1024,1536]{1,0:T(8,128)(2,1)} custom-call(s32[2]{0:T(128)} %get-tuple-element.77.which_ref, bf16[1024,256]{1,0:T(8,128)(2,1)} %copy-done.8, bf16[1024,256]{1,0:T(8,128)(2,1)} %copy-done.16, bf16[1024,256]{1,0:T(8,128)(2,1)} %copy-done.13, bf16[1024,256]{1,0:T(8,128)(2,1)} %copy-done.15, bf16[1024,256]{1,0:T(8,128)(2,1)} %copy-done.14, ...), custom_call_target="tpu_custom_call" | custom-call | flops 15000000512 | bytes 1048576 | tf_op jit(solution)/shard_map/pallas_call | solution.py:268
  (77 shorter events, 7.0 us)
Async XLA Ops:
  6.5 78.4 %copy-start.6 = (s32[4,3]{1,0:T(4,128)S(1)}, s32[4,3]{1,0:T(4,128)}, u32[]{:S(2)}) copy-start(s32[4,3]{1,0:T(4,128)} %constant.136.clone) | copy-start | bytes 148
  6.5 14.0 %copy-start.5 = (s32[1024]{0:T(1024)S(1)}, s32[1024]{0:T(1024)}, u32[]{:S(2)}) copy-start(s32[1024]{0:T(1024)} %param.11) | copy-start | bytes 12292
  6.5 23.1 %copy-start.4 = (s32[1024]{0:T(1024)S(1)}, s32[1024]{0:T(1024)}, u32[]{:S(2)}) copy-start(s32[1024]{0:T(1024)} %param.10) | copy-start | bytes 12292
  6.5 313.0 %all-gather.2.cloned.1.call-start = ((), (), s32[]{:S(2)}) async-start(), calls=%async_computation | async-start | bytes 10616832 | tf_op jit(solution)/shard_map/all_gather | solution.py:372
  6.5 76.2 %collective-permute-start = (bf16[1024,1536]{1,0:T(8,128)(2,1)}, bf16[1024,1536]{1,0:T(8,128)(2,1)}, u32[]{:S(2)}, u32[]{:S(2)}) collective-permute-start(bf16[1024,1536]{1,0:T(8,128)(2,1)} %refs_8_.1), channel_id=1, source_target_pairs={{1,2},{2,1},{5,6},{6,5},{9,10},{10,9},{13,14},{14,13},{17,18},{18,... | collective-permute-start | bytes 9437192 | tf_op jit(solution)/shard_map/ppermute | solution.py:54
  9.0 73.8 %collective-permute-start.1 = (bf16[1024,1536]{1,0:T(8,128)(2,1)}, bf16[1024,1536]{1,0:T(8,128)(2,1)}, u32[]{:S(2)}, u32[]{:S(2)}) collective-permute-start(bf16[1024,1536]{1,0:T(8,128)(2,1)} %refs_8_.1), channel_id=1, source_target_pairs={{0,1},{1,0},{2,3},{3,2},{4,5},{5,4},{6,7},{7,6},{8,9},{9,8},{10,11... | collective-permute-start | bytes 9437192 | tf_op jit(solution)/shard_map/ppermute | solution.py:54
  16.2 66.5 %collective-permute-start.2 = (f32[2,1024]{1,0:T(2,128)S(1)}, f32[2,1024]{1,0:T(2,128)S(1)}, u32[]{:S(2)}, u32[]{:S(2)}) collective-permute-start(f32[2,1024]{1,0:T(2,128)S(1)} %pad_maximum_fusion), channel_id=1, source_target_pairs={{0,1},{1,2},{2,3},{3,0},{4,5},{5,6},{6,7},{7,4},{8,9},{9,10},{10,1... | collective-permute-start | bytes 24584 | tf_op jit(solution)/shard_map/moments/ppermute | solution.py:325
  16.3 66.4 %collective-permute-start.3 = (f32[2,1024]{1,0:T(2,128)S(1)}, f32[2,1024]{1,0:T(2,128)S(1)}, u32[]{:S(2)}, u32[]{:S(2)}) collective-permute-start(f32[2,1024]{1,0:T(2,128)S(1)} %pad_maximum_fusion), channel_id=1, source_target_pairs={{0,2},{1,3},{2,0},{3,1},{4,6},{5,7},{6,4},{7,5},{8,10},{9,11},{10,... | collective-permute-start | bytes 24584 | tf_op jit(solution)/shard_map/moments/ppermute | solution.py:325
  18.2 64.5 %collective-permute-start.4 = (f32[2,1024]{1,0:T(2,128)S(1)}, f32[2,1024]{1,0:T(2,128)S(1)}, u32[]{:S(2)}, u32[]{:S(2)}) collective-permute-start(f32[2,1024]{1,0:T(2,128)S(1)} %pad_maximum_fusion), channel_id=1, source_target_pairs={{0,3},{1,0},{2,1},{3,2},{4,7},{5,4},{6,5},{7,6},{8,11},{9,8},{10,9... | collective-permute-start | bytes 24584 | tf_op jit(solution)/shard_map/moments/ppermute | solution.py:325
  35.8 120.3 %copy-start.3 = (s32[1024]{0:T(1024)}, s32[1024]{0:T(1024)S(1)}, u32[]{:S(2)}) copy-start(s32[1024]{0:T(1024)S(1)} %fusion.3) | copy-start | bytes 12292
  82.8 37.9 %collective-permute-start.5 = (bf16[1024,1536]{1,0:T(8,128)(2,1)}, bf16[1024,1536]{1,0:T(8,128)(2,1)S(1)}, u32[]{:S(2)}, u32[]{:S(2)}) collective-permute-start(bf16[1024,1536]{1,0:T(8,128)(2,1)} %collective-permute-done.1.refs_0_), channel_id=1, source_target_pairs={{1,2},{2,1},{5,6},{6,5},{9,10},{10,9},{13,14},{14,13},{17,18},{18,... | collective-permute-start | bytes 9437192 | tf_op jit(solution)/shard_map/ppermute | solution.py:54
  83.6 71.1 %collective-permute-start.6 = (bf16[1024,1536]{1,0:T(8,128)(2,1)}, bf16[1024,1536]{1,0:T(8,128)(2,1)}, u32[]{:S(2)}, u32[]{:S(2)}) collective-permute-start(bf16[1024,1536]{1,0:T(8,128)(2,1)} %collective-permute-done.refs_0_), channel_id=1, source_target_pairs={{1,0},{2,3},{5,4},{6,7},{9,8},{10,11},{13,12},{14,15},{17,16},{18,... | collective-permute-start | bytes 9437192 | tf_op jit(solution)/shard_map/ppermute | solution.py:54
  120.7 63.6 %copy-start = (bf16[1024,1536]{1,0:T(8,128)(2,1)}, bf16[1024,1536]{1,0:T(8,128)(2,1)S(1)}, u32[]{:S(2)}) copy-start(bf16[1024,1536]{1,0:T(8,128)(2,1)S(1)} %collective-permute-done.5.refs_0_) | copy-start | bytes 9437188
  154.7 85.1 %collective-permute-start.7 = (bf16[1024,1536]{1,0:T(8,128)(2,1)S(1)}, bf16[1024,1536]{1,0:T(8,128)(2,1)}, u32[]{:S(2)}, u32[]{:S(2)}) collective-permute-start(bf16[1024,1536]{1,0:T(8,128)(2,1)S(1)} %collective-permute-done.5.refs_0_), channel_id=1, source_target_pairs={{1,0},{2,3},{5,4},{6,7},{9,8},{10,11},{13,12},{14,15},{17,16},{18,... | collective-permute-start | bytes 9437192 | tf_op jit(solution)/shard_map/ppermute | solution.py:54
  159.1 95.6 %collective-permute-start.20 = (bf16[96,1536]{1,0:T(8,128)(2,1)S(1)}, bf16[96,1536]{1,0:T(8,128)(2,1)S(1)}, u32[]{:S(2)}, u32[]{:S(2)}) collective-permute-start(bf16[96,1536]{1,0:T(8,128)(2,1)S(1)} %get-tuple-element.69), channel_id=1, source_target_pairs={{0,1},{1,2},{2,3},{3,0},{4,5},{5,6},{6,7},{7,4},{8,9},{9,10},{10,1... | collective-permute-start | bytes 884744 | tf_op jit(solution)/shard_map/ppermute | solution.py:291
  163.4 91.3 %collective-permute-start.21 = (bf16[96,1536]{1,0:T(8,128)(2,1)S(1)}, bf16[96,1536]{1,0:T(8,128)(2,1)S(1)}, u32[]{:S(2)}, u32[]{:S(2)}) collective-permute-start(bf16[96,1536]{1,0:T(8,128)(2,1)S(1)} %get-tuple-element.68), channel_id=1, source_target_pairs={{0,2},{1,3},{2,0},{3,1},{4,6},{5,7},{6,4},{7,5},{8,10},{9,11},{10,... | collective-permute-start | bytes 884744 | tf_op jit(solution)/shard_map/ppermute | solution.py:291
  164.2 90.6 %collective-permute-start.22 = (bf16[96,1536]{1,0:T(8,128)(2,1)S(1)}, bf16[96,1536]{1,0:T(8,128)(2,1)S(1)}, u32[]{:S(2)}, u32[]{:S(2)}) collective-permute-start(bf16[96,1536]{1,0:T(8,128)(2,1)S(1)} %get-tuple-element.67), channel_id=1, source_target_pairs={{0,3},{1,0},{2,1},{3,2},{4,7},{5,4},{6,5},{7,6},{8,11},{9,8},{10,9... | collective-permute-start | bytes 884744 | tf_op jit(solution)/shard_map/ppermute | solution.py:291
  254.7 5.0 %copy-start.2 = (bf16[1024,256]{1,0:T(8,128)(2,1)S(1)}, bf16[1024,256]{1,0:T(8,128)(2,1)}, u32[]{:S(2)}) copy-start(bf16[1024,256]{1,0:T(8,128)(2,1)} %attend.3.refs_0_) | copy-start | bytes 1572868
  255.0 1.0 copy-start.1
  259.8 19.3 %collective-permute-start.8 = (bf16[1024,256]{1,0:T(8,128)(2,1)S(1)}, bf16[1024,256]{1,0:T(8,128)(2,1)S(1)}, u32[]{:S(2)}, u32[]{:S(2)}) collective-permute-start(bf16[1024,256]{1,0:T(8,128)(2,1)S(1)} %copy-done.2), channel_id=1, source_target_pairs={{1,2},{2,1},{5,6},{6,5},{9,10},{10,9},{13,14},{14,13},{17,18},{18,... | collective-permute-start | bytes 1572872 | tf_op jit(solution)/shard_map/ppermute | solution.py:54
  260.5 18.6 %collective-permute-start.9 = (bf16[1024,256]{1,0:T(8,128)(2,1)S(1)}, bf16[1024,256]{1,0:T(8,128)(2,1)S(1)}, u32[]{:S(2)}, u32[]{:S(2)}) collective-permute-start(bf16[1024,256]{1,0:T(8,128)(2,1)S(1)} %copy-done.2), channel_id=1, source_target_pairs={{0,1},{1,0},{2,3},{3,2},{4,5},{5,4},{6,7},{7,6},{8,9},{9,8},{10,11... | collective-permute-start | bytes 1572872 | tf_op jit(solution)/shard_map/ppermute | solution.py:54
  278.0 24.4 %collective-permute-start.13 = (bf16[1024,256]{1,0:T(8,128)(2,1)}, bf16[1024,256]{1,0:T(8,128)(2,1)S(1)}, u32[]{:S(2)}, u32[]{:S(2)}) collective-permute-start(bf16[1024,256]{1,0:T(8,128)(2,1)} %attend.4.refs_1_), channel_id=1, source_target_pairs={{0,1},{1,0},{2,3},{3,2},{4,5},{5,4},{6,7},{7,6},{8,9},{9,8},{10,11... | collective-permute-start | bytes 1572872 | tf_op jit(solution)/shard_map/ppermute | solution.py:54
  278.3 25.6 %collective-permute-start.12 = (bf16[1024,256]{1,0:T(8,128)(2,1)}, bf16[1024,256]{1,0:T(8,128)(2,1)S(1)}, u32[]{:S(2)}, u32[]{:S(2)}) collective-permute-start(bf16[1024,256]{1,0:T(8,128)(2,1)} %attend.4.refs_1_), channel_id=1, source_target_pairs={{1,2},{2,1},{5,6},{6,5},{9,10},{10,9},{13,14},{14,13},{17,18},{18,... | collective-permute-start | bytes 1572872 | tf_op jit(solution)/shard_map/ppermute | solution.py:54
  279.0 17.1 %copy-start.7 = (bf16[1024,256]{1,0:T(8,128)(2,1)}, bf16[1024,256]{1,0:T(8,128)(2,1)S(1)}, u32[]{:S(2)}) copy-start(bf16[1024,256]{1,0:T(8,128)(2,1)S(1)} %collective-permute-done.8.refs_0_) | copy-start | bytes 1572868
  279.1 17.1 %copy-start.10 = (bf16[1024,256]{1,0:T(8,128)(2,1)}, bf16[1024,256]{1,0:T(8,128)(2,1)S(1)}, u32[]{:S(2)}) copy-start(bf16[1024,256]{1,0:T(8,128)(2,1)S(1)} %collective-permute-done.9.refs_0_) | copy-start | bytes 1572868
  279.1 26.1 %collective-permute-start.10 = (bf16[1024,256]{1,0:T(8,128)(2,1)S(1)}, bf16[1024,256]{1,0:T(8,128)(2,1)S(1)}, u32[]{:S(2)}, u32[]{:S(2)}) collective-permute-start(bf16[1024,256]{1,0:T(8,128)(2,1)S(1)} %collective-permute-done.9.refs_0_), channel_id=1, source_target_pairs={{1,2},{2,1},{5,6},{6,5},{9,10},{10,9},{13,14},{14,13},{17,18},{18,... | collective-permute-start | bytes 1572872 | tf_op jit(solution)/shard_map/ppermute | solution.py:54
  279.8 26.2 %collective-permute-start.18 = (bf16[1024,256]{1,0:T(8,128)(2,1)S(1)}, bf16[1024,256]{1,0:T(8,128)(2,1)S(1)}, u32[]{:S(2)}, u32[]{:S(2)}) collective-permute-start(bf16[1024,256]{1,0:T(8,128)(2,1)S(1)} %collective-permute-done.8.refs_0_), channel_id=1, source_target_pairs={{1,0},{2,3},{5,4},{6,7},{9,8},{10,11},{13,12},{14,15},{17,16},{18,... | collective-permute-start | bytes 1572872 | tf_op jit(solution)/shard_map/ppermute | solution.py:54
  296.1 18.8 %collective-permute-start.17 = (bf16[1024,256]{1,0:T(8,128)(2,1)}, bf16[1024,256]{1,0:T(8,128)(2,1)}, u32[]{:S(2)}, u32[]{:S(2)}) collective-permute-start(bf16[1024,256]{1,0:T(8,128)(2,1)} %attend.5.refs_2_), channel_id=1, source_target_pairs={{0,1},{1,0},{2,3},{3,2},{4,5},{5,4},{6,7},{7,6},{8,9},{9,8},{10,11... | collective-permute-start | bytes 1572872 | tf_op jit(solution)/shard_map/ppermute | solution.py:54
  302.4 10.8 %copy-start.12 = (bf16[1024,256]{1,0:T(8,128)(2,1)}, bf16[1024,256]{1,0:T(8,128)(2,1)S(1)}, u32[]{:S(2)}) copy-start(bf16[1024,256]{1,0:T(8,128)(2,1)S(1)} %collective-permute-done.13.refs_1_) | copy-start | bytes 1572868
  302.4 12.5 %collective-permute-start.16 = (bf16[1024,256]{1,0:T(8,128)(2,1)}, bf16[1024,256]{1,0:T(8,128)(2,1)}, u32[]{:S(2)}, u32[]{:S(2)}) collective-permute-start(bf16[1024,256]{1,0:T(8,128)(2,1)} %attend.5.refs_2_), channel_id=1, source_target_pairs={{1,2},{2,1},{5,6},{6,5},{9,10},{10,9},{13,14},{14,13},{17,18},{18,... | collective-permute-start | bytes 1572872 | tf_op jit(solution)/shard_map/ppermute | solution.py:54
  303.9 9.3 %copy-start.9 = (bf16[1024,256]{1,0:T(8,128)(2,1)}, bf16[1024,256]{1,0:T(8,128)(2,1)S(1)}, u32[]{:S(2)}) copy-start(bf16[1024,256]{1,0:T(8,128)(2,1)S(1)} %collective-permute-done.12.refs_2_) | copy-start | bytes 1572868
  303.9 25.2 %collective-permute-start.24 = (bf16[1024,256]{1,0:T(8,128)(2,1)S(1)}, bf16[1024,256]{1,0:T(8,128)(2,1)}, u32[]{:S(2)}, u32[]{:S(2)}) collective-permute-start(bf16[1024,256]{1,0:T(8,128)(2,1)S(1)} %collective-permute-done.12.refs_2_), channel_id=1, source_target_pairs={{1,0},{2,3},{5,4},{6,7},{9,8},{10,11},{13,12},{14,15},{17,16},{18,... | collective-permute-start | bytes 1572872 | tf_op jit(solution)/shard_map/ppermute | solution.py:54
  305.2 13.0 %copy-start.8 = (bf16[1024,256]{1,0:T(8,128)(2,1)}, bf16[1024,256]{1,0:T(8,128)(2,1)S(1)}, u32[]{:S(2)}) copy-start(bf16[1024,256]{1,0:T(8,128)(2,1)S(1)} %collective-permute-done.10.refs_0_) | copy-start | bytes 1572868
  305.2 11.7 %collective-permute-start.14 = (bf16[1024,256]{1,0:T(8,128)(2,1)S(1)}, bf16[1024,256]{1,0:T(8,128)(2,1)S(1)}, u32[]{:S(2)}, u32[]{:S(2)}) collective-permute-start(bf16[1024,256]{1,0:T(8,128)(2,1)S(1)} %collective-permute-done.13.refs_1_), channel_id=1, source_target_pairs={{1,2},{2,1},{5,6},{6,5},{9,10},{10,9},{13,14},{14,13},{17,18},{18,... | collective-permute-start | bytes 1572872 | tf_op jit(solution)/shard_map/ppermute | solution.py:54
  305.9 7.3 %copy-start.11 = (bf16[1024,256]{1,0:T(8,128)(2,1)}, bf16[1024,256]{1,0:T(8,128)(2,1)S(1)}, u32[]{:S(2)}) copy-start(bf16[1024,256]{1,0:T(8,128)(2,1)S(1)} %collective-permute-done.18.refs_1_) | copy-start | bytes 1572868
  314.9 22.5 %collective-permute-start.25 = (bf16[1024,256]{1,0:T(8,128)(2,1)}, bf16[1024,256]{1,0:T(8,128)(2,1)}, u32[]{:S(2)}, u32[]{:S(2)}) collective-permute-start(bf16[1024,256]{1,0:T(8,128)(2,1)} %collective-permute-done.16.refs_4_), channel_id=1, source_target_pairs={{1,0},{2,3},{5,4},{6,7},{9,8},{10,11},{13,12},{14,15},{17,16},{18,... | collective-permute-start | bytes 1572872 | tf_op jit(solution)/shard_map/ppermute | solution.py:54
  316.2 11.6 %collective-permute-start.19 = (bf16[1024,256]{1,0:T(8,128)(2,1)}, bf16[1024,256]{1,0:T(8,128)(2,1)S(1)}, u32[]{:S(2)}, u32[]{:S(2)}) collective-permute-start(bf16[1024,256]{1,0:T(8,128)(2,1)} %collective-permute-done.17.refs_2_), channel_id=1, source_target_pairs={{1,2},{2,1},{5,6},{6,5},{9,10},{10,9},{13,14},{14,13},{17,18},{18,... | collective-permute-start | bytes 1572872 | tf_op jit(solution)/shard_map/ppermute | solution.py:54
  316.9 10.8 %copy-start.13 = (bf16[1024,256]{1,0:T(8,128)(2,1)}, bf16[1024,256]{1,0:T(8,128)(2,1)S(1)}, u32[]{:S(2)}) copy-start(bf16[1024,256]{1,0:T(8,128)(2,1)S(1)} %collective-permute-done.14.refs_2_) | copy-start | bytes 1572868
  316.9 31.6 %collective-permute-start.15 = (bf16[1024,256]{1,0:T(8,128)(2,1)S(1)}, bf16[1024,256]{1,0:T(8,128)(2,1)S(1)}, u32[]{:S(2)}, u32[]{:S(2)}) collective-permute-start(bf16[1024,256]{1,0:T(8,128)(2,1)S(1)} %collective-permute-done.14.refs_2_), channel_id=1, source_target_pairs={{1,0},{2,3},{5,4},{6,7},{9,8},{10,11},{13,12},{14,15},{17,16},{18,... | collective-permute-start | bytes 1572872 | tf_op jit(solution)/shard_map/ppermute | solution.py:54
  318.3 39.7 %collective-permute-start.11 = (bf16[1024,256]{1,0:T(8,128)(2,1)S(1)}, bf16[1024,256]{1,0:T(8,128)(2,1)S(1)}, u32[]{:S(2)}, u32[]{:S(2)}) collective-permute-start(bf16[1024,256]{1,0:T(8,128)(2,1)S(1)} %collective-permute-done.10.refs_0_), channel_id=1, source_target_pairs={{1,0},{2,3},{5,4},{6,7},{9,8},{10,11},{13,12},{14,15},{17,16},{18,... | collective-permute-start | bytes 1572872 | tf_op jit(solution)/shard_map/ppermute | solution.py:54
  327.8 18.1 %copy-start.14 = (bf16[1024,256]{1,0:T(8,128)(2,1)}, bf16[1024,256]{1,0:T(8,128)(2,1)S(1)}, u32[]{:S(2)}) copy-start(bf16[1024,256]{1,0:T(8,128)(2,1)S(1)} %collective-permute-done.19.refs_4_) | copy-start | bytes 1572868
  327.8 35.8 %collective-permute-start.23 = (bf16[1024,256]{1,0:T(8,128)(2,1)S(1)}, bf16[1024,256]{1,0:T(8,128)(2,1)S(1)}, u32[]{:S(2)}, u32[]{:S(2)}) collective-permute-start(bf16[1024,256]{1,0:T(8,128)(2,1)S(1)} %collective-permute-done.19.refs_4_), channel_id=1, source_target_pairs={{1,0},{2,3},{5,4},{6,7},{9,8},{10,11},{13,12},{14,15},{17,16},{18,... | collective-permute-start | bytes 1572872 | tf_op jit(solution)/shard_map/ppermute | solution.py:54
  348.5 15.0 %copy-start.15 = (bf16[1024,256]{1,0:T(8,128)(2,1)}, bf16[1024,256]{1,0:T(8,128)(2,1)S(1)}, u32[]{:S(2)}) copy-start(bf16[1024,256]{1,0:T(8,128)(2,1)S(1)} %collective-permute-done.15.refs_3_) | copy-start | bytes 1572868
  357.9 5.6 %copy-start.16 = (bf16[1024,256]{1,0:T(8,128)(2,1)}, bf16[1024,256]{1,0:T(8,128)(2,1)S(1)}, u32[]{:S(2)}) copy-start(bf16[1024,256]{1,0:T(8,128)(2,1)S(1)} %collective-permute-done.11.refs_1_) | copy-start | bytes 1572868
  363.6 0.8 copy-start.17
Sparse Core Ops, SparseCore 0:
  256.2 58.6 all-gather.1

commit v2 on v1

--- a/solution.py
+++ b/solution.py
@@ -145,9 +145,9 @@
     rows, depth = parts[0].shape
     kinds = weight.shape[0]
     cols = heads * HEAD_DIM
-    deep = pick(depth, 512)
+    deep = pick(depth, 768)
     steps = depth // deep
-    tile = pick(rows, 256)
+    tile = pick(rows, 512)
     scale = math.log2(math.e) / math.sqrt(HEAD_DIM)
     count = len(parts)
 

time: 381 us -> 380 us (level)
  no operation moved by 1% of the time
where the time goes in v2:
time: 380 us; the launch traced here: 379 us
  waiting for transfers between devices  164 us (43%)
  Pallas kernels  124 us (33%)
  starting transfers between devices  43.7 us (12%)
  local copies, waits for them, and re-layouts  14.9 us (4%)
  between operations  13.9 us (4%)
  blocking collectives  9.07 us (2%)
  other arithmetic  8.74 us (2%)
    ppermute x20, waiting for transfers between devices, step(): self.got[s, kind] = lax.ppermute(source, self.axis, self.steps[s, kind])  117 us
    pallas_call x3, Pallas kernels, project(): pl.pallas_call(kernel, grid_spec=pltpu.PrefetchScalarGridSpec(num_scalar_...  47.2 us
    ppermute x3, waiting for transfers between devices, shards(): lax.ppermute(moments, 'mp', [(i, (i + d) % n) for i in range(n)])  46.9 us
    pallas_call x3, Pallas kernels, attend(): pl.pallas_call(kernel, grid_spec=pltpu.PrefetchScalarGridSpec(num_scalar_...  44.6 us
    pallas_call x4, Pallas kernels, project_out(): pl.pallas_call(kernel, grid_spec=pltpu.PrefetchScalarGridSpec(num_scalar_...  32.6 us
    ppermute x20, starting transfers between devices, step(): self.got[s, kind] = lax.ppermute(source, self.axis, self.steps[s, kind])  31.5 us
    all_gather x1, blocking collectives, shards(): segment = lax.all_gather(segment_ids, 'dp', tiled=True)[dest_pos]  9.07 us
    ppermute x3, starting transfers between devices, exchange_out_weight(): lax.ppermute(columns((place + d) % n), 'mp', [(i, (i + d) % n) for i in r...  7.86 us
  transfers between devices with their start and end apart: 27, of which 8 were waited for; matrix products, arithmetic and copies ran while one was open for 6% of the time, Pallas kernels for 31%

profile of v2, /device:TPU:0, one launch (start us, length us, event | category | flops | bytes accessed | tf_op | source)
XLA Modules:
  0.0 379.1 jit_solution(11960756153034588840)
XLA Ops:
  6.5 2.4 collective-permute-start
  9.0 4.3 %collective-permute-start.1 = (bf16[1024,1536]{1,0:T(8,128)(2,1)}, bf16[1024,1536]{1,0:T(8,128)(2,1)}, u32[]{:S(2)}, u32[]{:S(2)}) collective-permute-start(bf16[1024,1536]{1,0:T(8,128)(2,1)} %refs_8_.1), channel_id=1, source_target_pairs={{0,1},{1,0},{2,3},{3,2},{4,5},{5,4},{6,7},{7,6},{8,9},{9,8},{10,11... | collective-permute-start | bytes 9437192 | tf_op jit(solution)/shard_map/ppermute | solution.py:54
  13.3 2.9 convert_reduce_fusion
  16.3 1.9 collective-permute-start.3
  18.2 2.4 collective-permute-start.4
  20.5 9.1 %all_gather.6 = s32[8192]{0:T(1024)S(1)} all-gather(s32[1024]{0:T(1024)S(1)} %copy-done.5), channel_id=1, replica_groups=mesh['dp'=8,'mp'=4] {'dp'}, dimensions={0}, use_global_device_ids=true | all-gather | bytes 36864 | tf_op jit(solution)/shard_map/all_gather | solution.py:314
  29.6 6.1 %gather_fusion = s32[1024]{0:T(1024)S(1)} fusion(s32[8192]{0:T(1024)S(1)} %all_gather.6, s32[1024]{0:T(1024)S(1)} %fusion.4), kind=kCustom, calls=%fused_computation | custom fusion | bytes 12288 | tf_op jit(solution)/shard_map/gather | solution.py:314
  35.8 46.9 %collective-permute-done.2 = f32[2,1024]{1,0:T(2,128)S(1)} collective-permute-done((f32[2,1024]{1,0:T(2,128)S(1)}, f32[2,1024]{1,0:T(2,128)S(1)}, u32[]{:S(2)}, u32[]{:S(2)}) %collective-permute-start.2) | collective-permute-done | bytes 8224 | tf_op jit(solution)/shard_map/moments/ppermute | solution.py:325
  82.8 0.9 collective-permute-start.5
  83.6 1.3 collective-permute-start.6
  85.6 1.0 copy.35
  86.6 1.0 copy.36
  87.6 1.0 copy.38.refs_1_.refs_2_
  88.7 2.1 add_rsqrt_fusion.refs_2_.refs_3_
  90.7 13.6 %project.3.refs_5_ = f32[3,1024,768]{2,1,0:T(8,128)} custom-call(s32[1]{0:T(128)} %bitcast.7.which_ref, bf16[1024,1536]{1,0:T(8,128)(2,1)} %refs_8_.1, f32[1024,1]{1,0:T(8,128)} %copy.38.refs_1_.refs_2_, f32[1024,1]{1,0:T(8,128)} %add_rsqrt_fusion.refs_2_.refs_3_, f32[1,6144]{1,0:T(1,128)} %bitcast.25, bf16[3,6144,768]{2,1,0:T(8,128)(2,1)} %refs_7_.5), custom_call_target="tpu_custom_call" | custom-call | flops 7247757312 | bytes 25952256 | tf_op jit(solution)/shard_map/project/pallas_call | solution.py:117
  104.3 16.4 %project.4.refs_6_ = f32[3,1024,768]{2,1,0:T(8,128)} custom-call(s32[1]{0:T(128)} %bitcast.3.which_ref, bf16[1024,1536]{1,0:T(8,128)(2,1)} %collective-permute-done.1.refs_0_, f32[1024,1]{1,0:T(8,128)} %copy.38.refs_1_.refs_2_, f32[1024,1]{1,0:T(8,128)} %add_rsqrt_fusion.refs_2_.refs_3_, f32[1,6144]{1,0:T(1,128)} %bitcast.26, ...), custom_call_target="tpu_custom_call", output_to_operand_aliasing={{}: (6, {})} | custom-call | flops 7247757312 | bytes 25952256 | tf_op jit(solution)/shard_map/project/pallas_call | solution.py:117
  120.7 34.1 %collective-permute-done.6.refs_1_ = bf16[1024,1536]{1,0:T(8,128)(2,1)} collective-permute-done((bf16[1024,1536]{1,0:T(8,128)(2,1)}, bf16[1024,1536]{1,0:T(8,128)(2,1)}, u32[]{:S(2)}, u32[]{:S(2)}) %collective-permute-start.6) | collective-permute-done | bytes 3145760 | tf_op jit(solution)/shard_map/ppermute | solution.py:54
  154.7 1.3 collective-permute-start.7
  156.1 1.0 copy.41.refs_12_
  157.2 2.0 fusion.7
  159.1 4.3 %collective-permute-start.20 = (bf16[96,1536]{1,0:T(8,128)(2,1)S(1)}, bf16[96,1536]{1,0:T(8,128)(2,1)S(1)}, u32[]{:S(2)}, u32[]{:S(2)}) collective-permute-start(bf16[96,1536]{1,0:T(8,128)(2,1)S(1)} %get-tuple-element.69), channel_id=1, source_target_pairs={{0,1},{1,2},{2,3},{3,0},{4,5},{5,6},{6,7},{7,4},{8,9},{9,10},{10,1... | collective-permute-start | bytes 884744 | tf_op jit(solution)/shard_map/ppermute | solution.py:291
  164.2 2.8 collective-permute-start.22
  167.0 17.2 %project.5.refs_8_.refs_9_.refs_10_ = f32[3,1024,768]{2,1,0:T(8,128)} custom-call(s32[1]{0:T(128)} %bitcast.8.which_ref, bf16[1024,1536]{1,0:T(8,128)(2,1)} %collective-permute-done.refs_0_, bf16[1024,1536]{1,0:T(8,128)(2,1)} %collective-permute-done.6.refs_1_, f32[1024,1]{1,0:T(8,128)} %copy.38.refs_1_.refs_2_, ...), custom_call_target="tpu_custom_call", output_to_operand_aliasing={{}: (7, {})} | custom-call | flops 7247757312 | bytes 25952256 | tf_op jit(solution)/shard_map/project/pallas_call | solution.py:117
  184.2 55.6 %collective-permute-done.7.refs_1_ = bf16[1024,1536]{1,0:T(8,128)(2,1)} collective-permute-done((bf16[1024,1536]{1,0:T(8,128)(2,1)S(1)}, bf16[1024,1536]{1,0:T(8,128)(2,1)}, u32[]{:S(2)}, u32[]{:S(2)}) %collective-permute-start.7) | collective-permute-done | bytes 3145760 | tf_op jit(solution)/shard_map/ppermute | solution.py:54
  239.9 14.5 %attend.3.refs_0_ = bf16[1024,256]{1,0:T(8,128)(2,1)} custom-call(s32[1]{0:T(128)} %bitcast.which_ref, bf16[1024,1536]{1,0:T(8,128)(2,1)} %copy-done, bf16[1024,1536]{1,0:T(8,128)(2,1)} %collective-permute-done.7.refs_1_, f32[1024,1]{1,0:T(8,128)} %copy.38.refs_1_.refs_2_, f32[1024,1]{1,0:T(8,128)} %add_rsqrt_fusion.refs_2_.refs_3_, f32[1,6144]{1,0:T(1,128)} %bitcast.28, ...), custom_call_target="tpu_custom_call" | custom-call | flops 15000000512 | bytes 1048576 | tf_op jit(solution)/shard_map/attend/pallas_call | solution.py:217
  254.7 1.0 copy-done.1
  256.3 1.3 pad_add_fusion.1.which_ref
  257.6 1.8 pad_add_fusion
  260.1 2.0 collective-permute-start.9
  262.1 15.2 %attend.4.refs_1_ = bf16[1024,256]{1,0:T(8,128)(2,1)} custom-call(s32[1]{0:T(128)} %bitcast.which_ref, bf16[1024,1536]{1,0:T(8,128)(2,1)} %copy-done, bf16[1024,1536]{1,0:T(8,128)(2,1)} %collective-permute-done.7.refs_1_, f32[1024,1]{1,0:T(8,128)} %copy.38.refs_1_.refs_2_, f32[1024,1]{1,0:T(8,128)} %add_rsqrt_fusion.refs_2_.refs_3_, f32[1,6144]{1,0:T(1,128)} %bitcast.29, ...), custom_call_target="tpu_custom_call" | custom-call | flops 15000000512 | bytes 1048576 | tf_op jit(solution)/shard_map/attend/pallas_call | solution.py:217
  279.3 1.5 collective-permute-start.18
  280.8 14.9 %attend.5.refs_2_ = bf16[1024,256]{1,0:T(8,128)(2,1)} custom-call(s32[1]{0:T(128)} %bitcast.which_ref, bf16[1024,1536]{1,0:T(8,128)(2,1)} %copy-done, bf16[1024,1536]{1,0:T(8,128)(2,1)} %collective-permute-done.7.refs_1_, f32[1024,1]{1,0:T(8,128)} %copy.38.refs_1_.refs_2_, f32[1024,1]{1,0:T(8,128)} %add_rsqrt_fusion.refs_2_.refs_3_, f32[1,6144]{1,0:T(1,128)} %bitcast.30, ...), custom_call_target="tpu_custom_call" | custom-call | flops 15000000512 | bytes 1048576 | tf_op jit(solution)/shard_map/attend/pallas_call | solution.py:217
  295.8 5.9 %collective-permute-start.17 = (bf16[1024,256]{1,0:T(8,128)(2,1)}, bf16[1024,256]{1,0:T(8,128)(2,1)}, u32[]{:S(2)}, u32[]{:S(2)}) collective-permute-start(bf16[1024,256]{1,0:T(8,128)(2,1)} %attend.5.refs_2_), channel_id=1, source_target_pairs={{0,1},{1,0},{2,3},{3,2},{4,5},{5,4},{6,7},{7,6},{8,9},{9,8},{10,11... | collective-permute-start | bytes 1572872 | tf_op jit(solution)/shard_map/ppermute | solution.py:54
  301.6 1.5 collective-permute-start.16
  303.1 1.3 collective-permute-start.24
  305.2 7.2 %shard_map.82.refs_4_ = f32[1024,1536]{1,0:T(8,128)} custom-call(s32[2]{0:T(128)} %pad_add_fusion.3.which_ref, bf16[1024,256]{1,0:T(8,128)(2,1)} %attend.3.refs_0_, bf16[1024,256]{1,0:T(8,128)(2,1)} %attend.4.refs_1_, bf16[1024,256]{1,0:T(8,128)(2,1)} %attend.5.refs_2_, bf16[1,768,6144]{2,1,0:T(8,128)(2,1)} %bitcast.31), custom_call_target="tpu_custom_call" | custom-call | flops 15000000512 | bytes 1048576 | tf_op jit(solution)/shard_map/pallas_call | solution.py:268
  312.4 2.0 collective-permute-done.17.refs_2_
  314.4 1.3 collective-permute-start.25
  316.4 1.3 collective-permute-start.15
  317.8 1.3 collective-permute-start.11
  319.1 8.2 %shard_map.83.refs_7_ = f32[1024,1536]{1,0:T(8,128)} custom-call(s32[2]{0:T(128)} %pad_add_fusion.1.which_ref, bf16[1024,256]{1,0:T(8,128)(2,1)} %copy-done.10, bf16[1024,256]{1,0:T(8,128)(2,1)} %copy-done.12, bf16[1024,256]{1,0:T(8,128)(2,1)} %collective-permute-done.17.refs_2_, bf16[4,768,1536]{2,1,0:T(8,128)(2,1)} %all-gather.2.cloned.1.call-done.refs_3_.refs_6_, ...), custom_call_target="tpu_custom_call" | custom-call | flops 15000000512 | bytes 1048576 | tf_op jit(solution)/shard_map/pallas_call | solution.py:268
  327.3 1.3 collective-permute-start.23
  328.6 8.3 %collective-permute-done.25.refs_5_ = bf16[1024,256]{1,0:T(8,128)(2,1)} collective-permute-done((bf16[1024,256]{1,0:T(8,128)(2,1)}, bf16[1024,256]{1,0:T(8,128)(2,1)}, u32[]{:S(2)}, u32[]{:S(2)}) %collective-permute-start.25) | collective-permute-done | bytes 524320 | tf_op jit(solution)/shard_map/ppermute | solution.py:54
  336.9 8.5 %shard_map.84.refs_7_ = f32[1024,1536]{1,0:T(8,128)} custom-call(s32[2]{0:T(128)} %get-tuple-element.76.which_ref, bf16[1024,256]{1,0:T(8,128)(2,1)} %copy-done.7, bf16[1024,256]{1,0:T(8,128)(2,1)} %copy-done.11, bf16[1024,256]{1,0:T(8,128)(2,1)} %copy-done.9, bf16[1024,256]{1,0:T(8,128)(2,1)} %collective-permute-done.24.refs_3_, ...), custom_call_target="tpu_custom_call" | custom-call | flops 15000000512 | bytes 1048576 | tf_op jit(solution)/shard_map/pallas_call | solution.py:268
  345.4 2.6 collective-permute-done.15.refs_3_
  348.0 9.2 %collective-permute-done.11.refs_1_ = bf16[1024,256]{1,0:T(8,128)(2,1)S(1)} collective-permute-done((bf16[1024,256]{1,0:T(8,128)(2,1)S(1)}, bf16[1024,256]{1,0:T(8,128)(2,1)S(1)}, u32[]{:S(2)}, u32[]{:S(2)}) %collective-permute-start.11) | collective-permute-done | bytes 524320 | tf_op jit(solution)/shard_map/ppermute | solution.py:54
  357.2 5.6 %collective-permute-done.23.refs_5_ = bf16[1024,256]{1,0:T(8,128)(2,1)S(1)} collective-permute-done((bf16[1024,256]{1,0:T(8,128)(2,1)S(1)}, bf16[1024,256]{1,0:T(8,128)(2,1)S(1)}, u32[]{:S(2)}, u32[]{:S(2)}) %collective-permute-start.23) | collective-permute-done | bytes 524320 | tf_op jit(solution)/shard_map/ppermute | solution.py:54
  363.7 8.6 %shard_map.85 = bf16[1024,1536]{1,0:T(8,128)(2,1)} custom-call(s32[2]{0:T(128)} %get-tuple-element.77.which_ref, bf16[1024,256]{1,0:T(8,128)(2,1)} %copy-done.8, bf16[1024,256]{1,0:T(8,128)(2,1)} %copy-done.16, bf16[1024,256]{1,0:T(8,128)(2,1)} %copy-done.13, bf16[1024,256]{1,0:T(8,128)(2,1)} %copy-done.15, bf16[1024,256]{1,0:T(8,128)(2,1)} %copy-done.14, ...), custom_call_target="tpu_custom_call" | custom-call | flops 15000000512 | bytes 1048576 | tf_op jit(solution)/shard_map/pallas_call | solution.py:268
  (77 shorter events, 7.2 us)
Async XLA Ops:
  6.5 78.4 %copy-start.6 = (s32[4,3]{1,0:T(4,128)S(1)}, s32[4,3]{1,0:T(4,128)}, u32[]{:S(2)}) copy-start(s32[4,3]{1,0:T(4,128)} %constant.136.clone) | copy-start | bytes 148
  6.5 14.0 %copy-start.5 = (s32[1024]{0:T(1024)S(1)}, s32[1024]{0:T(1024)}, u32[]{:S(2)}) copy-start(s32[1024]{0:T(1024)} %param.11) | copy-start | bytes 12292
  6.5 23.1 %copy-start.4 = (s32[1024]{0:T(1024)S(1)}, s32[1024]{0:T(1024)}, u32[]{:S(2)}) copy-start(s32[1024]{0:T(1024)} %param.10) | copy-start | bytes 12292
  6.5 312.5 %all-gather.2.cloned.1.call-start = ((), (), s32[]{:S(2)}) async-start(), calls=%async_computation | async-start | bytes 10616832 | tf_op jit(solution)/shard_map/all_gather | solution.py:372
  6.5 76.2 %collective-permute-start = (bf16[1024,1536]{1,0:T(8,128)(2,1)}, bf16[1024,1536]{1,0:T(8,128)(2,1)}, u32[]{:S(2)}, u32[]{:S(2)}) collective-permute-start(bf16[1024,1536]{1,0:T(8,128)(2,1)} %refs_8_.1), channel_id=1, source_target_pairs={{1,2},{2,1},{5,6},{6,5},{9,10},{10,9},{13,14},{14,13},{17,18},{18,... | collective-permute-start | bytes 9437192 | tf_op jit(solution)/shard_map/ppermute | solution.py:54
  9.0 73.8 %collective-permute-start.1 = (bf16[1024,1536]{1,0:T(8,128)(2,1)}, bf16[1024,1536]{1,0:T(8,128)(2,1)}, u32[]{:S(2)}, u32[]{:S(2)}) collective-permute-start(bf16[1024,1536]{1,0:T(8,128)(2,1)} %refs_8_.1), channel_id=1, source_target_pairs={{0,1},{1,0},{2,3},{3,2},{4,5},{5,4},{6,7},{7,6},{8,9},{9,8},{10,11... | collective-permute-start | bytes 9437192 | tf_op jit(solution)/shard_map/ppermute | solution.py:54
  16.2 66.5 %collective-permute-start.2 = (f32[2,1024]{1,0:T(2,128)S(1)}, f32[2,1024]{1,0:T(2,128)S(1)}, u32[]{:S(2)}, u32[]{:S(2)}) collective-permute-start(f32[2,1024]{1,0:T(2,128)S(1)} %pad_maximum_fusion), channel_id=1, source_target_pairs={{0,1},{1,2},{2,3},{3,0},{4,5},{5,6},{6,7},{7,4},{8,9},{9,10},{10,1... | collective-permute-start | bytes 24584 | tf_op jit(solution)/shard_map/moments/ppermute | solution.py:325
  16.3 66.4 %collective-permute-start.3 = (f32[2,1024]{1,0:T(2,128)S(1)}, f32[2,1024]{1,0:T(2,128)S(1)}, u32[]{:S(2)}, u32[]{:S(2)}) collective-permute-start(f32[2,1024]{1,0:T(2,128)S(1)} %pad_maximum_fusion), channel_id=1, source_target_pairs={{0,2},{1,3},{2,0},{3,1},{4,6},{5,7},{6,4},{7,5},{8,10},{9,11},{10,... | collective-permute-start | bytes 24584 | tf_op jit(solution)/shard_map/moments/ppermute | solution.py:325
  18.2 64.5 %collective-permute-start.4 = (f32[2,1024]{1,0:T(2,128)S(1)}, f32[2,1024]{1,0:T(2,128)S(1)}, u32[]{:S(2)}, u32[]{:S(2)}) collective-permute-start(f32[2,1024]{1,0:T(2,128)S(1)} %pad_maximum_fusion), channel_id=1, source_target_pairs={{0,3},{1,0},{2,1},{3,2},{4,7},{5,4},{6,5},{7,6},{8,11},{9,8},{10,9... | collective-permute-start | bytes 24584 | tf_op jit(solution)/shard_map/moments/ppermute | solution.py:325
  35.8 120.3 %copy-start.3 = (s32[1024]{0:T(1024)}, s32[1024]{0:T(1024)S(1)}, u32[]{:S(2)}) copy-start(s32[1024]{0:T(1024)S(1)} %fusion.3) | copy-start | bytes 12292
  82.8 37.9 %collective-permute-start.5 = (bf16[1024,1536]{1,0:T(8,128)(2,1)}, bf16[1024,1536]{1,0:T(8,128)(2,1)S(1)}, u32[]{:S(2)}, u32[]{:S(2)}) collective-permute-start(bf16[1024,1536]{1,0:T(8,128)(2,1)} %collective-permute-done.1.refs_0_), channel_id=1, source_target_pairs={{1,2},{2,1},{5,6},{6,5},{9,10},{10,9},{13,14},{14,13},{17,18},{18,... | collective-permute-start | bytes 9437192 | tf_op jit(solution)/shard_map/ppermute | solution.py:54
  83.6 71.1 %collective-permute-start.6 = (bf16[1024,1536]{1,0:T(8,128)(2,1)}, bf16[1024,1536]{1,0:T(8,128)(2,1)}, u32[]{:S(2)}, u32[]{:S(2)}) collective-permute-start(bf16[1024,1536]{1,0:T(8,128)(2,1)} %collective-permute-done.refs_0_), channel_id=1, source_target_pairs={{1,0},{2,3},{5,4},{6,7},{9,8},{10,11},{13,12},{14,15},{17,16},{18,... | collective-permute-start | bytes 9437192 | tf_op jit(solution)/shard_map/ppermute | solution.py:54
  120.7 63.6 %copy-start = (bf16[1024,1536]{1,0:T(8,128)(2,1)}, bf16[1024,1536]{1,0:T(8,128)(2,1)S(1)}, u32[]{:S(2)}) copy-start(bf16[1024,1536]{1,0:T(8,128)(2,1)S(1)} %collective-permute-done.5.refs_0_) | copy-start | bytes 9437188
  154.7 85.1 %collective-permute-start.7 = (bf16[1024,1536]{1,0:T(8,128)(2,1)S(1)}, bf16[1024,1536]{1,0:T(8,128)(2,1)}, u32[]{:S(2)}, u32[]{:S(2)}) collective-permute-start(bf16[1024,1536]{1,0:T(8,128)(2,1)S(1)} %collective-permute-done.5.refs_0_), channel_id=1, source_target_pairs={{1,0},{2,3},{5,4},{6,7},{9,8},{10,11},{13,12},{14,15},{17,16},{18,... | collective-permute-start | bytes 9437192 | tf_op jit(solution)/shard_map/ppermute | solution.py:54
  159.1 95.2 %collective-permute-start.20 = (bf16[96,1536]{1,0:T(8,128)(2,1)S(1)}, bf16[96,1536]{1,0:T(8,128)(2,1)S(1)}, u32[]{:S(2)}, u32[]{:S(2)}) collective-permute-start(bf16[96,1536]{1,0:T(8,128)(2,1)S(1)} %get-tuple-element.69), channel_id=1, source_target_pairs={{0,1},{1,2},{2,3},{3,0},{4,5},{5,6},{6,7},{7,4},{8,9},{9,10},{10,1... | collective-permute-start | bytes 884744 | tf_op jit(solution)/shard_map/ppermute | solution.py:291
  163.4 91.0 %collective-permute-start.21 = (bf16[96,1536]{1,0:T(8,128)(2,1)S(1)}, bf16[96,1536]{1,0:T(8,128)(2,1)S(1)}, u32[]{:S(2)}, u32[]{:S(2)}) collective-permute-start(bf16[96,1536]{1,0:T(8,128)(2,1)S(1)} %get-tuple-element.68), channel_id=1, source_target_pairs={{0,2},{1,3},{2,0},{3,1},{4,6},{5,7},{6,4},{7,5},{8,10},{9,11},{10,... | collective-permute-start | bytes 884744 | tf_op jit(solution)/shard_map/ppermute | solution.py:291
  164.2 90.3 %collective-permute-start.22 = (bf16[96,1536]{1,0:T(8,128)(2,1)S(1)}, bf16[96,1536]{1,0:T(8,128)(2,1)S(1)}, u32[]{:S(2)}, u32[]{:S(2)}) collective-permute-start(bf16[96,1536]{1,0:T(8,128)(2,1)S(1)} %get-tuple-element.67), channel_id=1, source_target_pairs={{0,3},{1,0},{2,1},{3,2},{4,7},{5,4},{6,5},{7,6},{8,11},{9,8},{10,9... | collective-permute-start | bytes 884744 | tf_op jit(solution)/shard_map/ppermute | solution.py:291
  254.4 5.0 %copy-start.2 = (bf16[1024,256]{1,0:T(8,128)(2,1)S(1)}, bf16[1024,256]{1,0:T(8,128)(2,1)}, u32[]{:S(2)}) copy-start(bf16[1024,256]{1,0:T(8,128)(2,1)} %attend.3.refs_0_) | copy-start | bytes 1572868
  254.6 1.0 copy-start.1
  259.4 19.2 %collective-permute-start.8 = (bf16[1024,256]{1,0:T(8,128)(2,1)S(1)}, bf16[1024,256]{1,0:T(8,128)(2,1)S(1)}, u32[]{:S(2)}, u32[]{:S(2)}) collective-permute-start(bf16[1024,256]{1,0:T(8,128)(2,1)S(1)} %copy-done.2), channel_id=1, source_target_pairs={{1,2},{2,1},{5,6},{6,5},{9,10},{10,9},{13,14},{14,13},{17,18},{18,... | collective-permute-start | bytes 1572872 | tf_op jit(solution)/shard_map/ppermute | solution.py:54
  260.1 18.5 %collective-permute-start.9 = (bf16[1024,256]{1,0:T(8,128)(2,1)S(1)}, bf16[1024,256]{1,0:T(8,128)(2,1)S(1)}, u32[]{:S(2)}, u32[]{:S(2)}) collective-permute-start(bf16[1024,256]{1,0:T(8,128)(2,1)S(1)} %copy-done.2), channel_id=1, source_target_pairs={{0,1},{1,0},{2,3},{3,2},{4,5},{5,4},{6,7},{7,6},{8,9},{9,8},{10,11... | collective-permute-start | bytes 1572872 | tf_op jit(solution)/shard_map/ppermute | solution.py:54
  277.3 24.3 %collective-permute-start.13 = (bf16[1024,256]{1,0:T(8,128)(2,1)}, bf16[1024,256]{1,0:T(8,128)(2,1)S(1)}, u32[]{:S(2)}, u32[]{:S(2)}) collective-permute-start(bf16[1024,256]{1,0:T(8,128)(2,1)} %attend.4.refs_1_), channel_id=1, source_target_pairs={{0,1},{1,0},{2,3},{3,2},{4,5},{5,4},{6,7},{7,6},{8,9},{9,8},{10,11... | collective-permute-start | bytes 1572872 | tf_op jit(solution)/shard_map/ppermute | solution.py:54
  277.9 25.3 %collective-permute-start.12 = (bf16[1024,256]{1,0:T(8,128)(2,1)}, bf16[1024,256]{1,0:T(8,128)(2,1)S(1)}, u32[]{:S(2)}, u32[]{:S(2)}) collective-permute-start(bf16[1024,256]{1,0:T(8,128)(2,1)} %attend.4.refs_1_), channel_id=1, source_target_pairs={{1,2},{2,1},{5,6},{6,5},{9,10},{10,9},{13,14},{14,13},{17,18},{18,... | collective-permute-start | bytes 1572872 | tf_op jit(solution)/shard_map/ppermute | solution.py:54
  278.6 17.2 %copy-start.7 = (bf16[1024,256]{1,0:T(8,128)(2,1)}, bf16[1024,256]{1,0:T(8,128)(2,1)S(1)}, u32[]{:S(2)}) copy-start(bf16[1024,256]{1,0:T(8,128)(2,1)S(1)} %collective-permute-done.8.refs_0_) | copy-start | bytes 1572868
  278.6 17.2 %copy-start.10 = (bf16[1024,256]{1,0:T(8,128)(2,1)}, bf16[1024,256]{1,0:T(8,128)(2,1)S(1)}, u32[]{:S(2)}) copy-start(bf16[1024,256]{1,0:T(8,128)(2,1)S(1)} %collective-permute-done.9.refs_0_) | copy-start | bytes 1572868
  278.6 25.8 %collective-permute-start.10 = (bf16[1024,256]{1,0:T(8,128)(2,1)S(1)}, bf16[1024,256]{1,0:T(8,128)(2,1)S(1)}, u32[]{:S(2)}, u32[]{:S(2)}) collective-permute-start(bf16[1024,256]{1,0:T(8,128)(2,1)S(1)} %collective-permute-done.9.refs_0_), channel_id=1, source_target_pairs={{1,2},{2,1},{5,6},{6,5},{9,10},{10,9},{13,14},{14,13},{17,18},{18,... | collective-permute-start | bytes 1572872 | tf_op jit(solution)/shard_map/ppermute | solution.py:54
  279.3 25.8 %collective-permute-start.18 = (bf16[1024,256]{1,0:T(8,128)(2,1)S(1)}, bf16[1024,256]{1,0:T(8,128)(2,1)S(1)}, u32[]{:S(2)}, u32[]{:S(2)}) collective-permute-start(bf16[1024,256]{1,0:T(8,128)(2,1)S(1)} %collective-permute-done.8.refs_0_), channel_id=1, source_target_pairs={{1,0},{2,3},{5,4},{6,7},{9,8},{10,11},{13,12},{14,15},{17,16},{18,... | collective-permute-start | bytes 1572872 | tf_op jit(solution)/shard_map/ppermute | solution.py:54
  295.8 18.7 %collective-permute-start.17 = (bf16[1024,256]{1,0:T(8,128)(2,1)}, bf16[1024,256]{1,0:T(8,128)(2,1)}, u32[]{:S(2)}, u32[]{:S(2)}) collective-permute-start(bf16[1024,256]{1,0:T(8,128)(2,1)} %attend.5.refs_2_), channel_id=1, source_target_pairs={{0,1},{1,0},{2,3},{3,2},{4,5},{5,4},{6,7},{7,6},{8,9},{9,8},{10,11... | collective-permute-start | bytes 1572872 | tf_op jit(solution)/shard_map/ppermute | solution.py:54
  301.6 10.8 %copy-start.12 = (bf16[1024,256]{1,0:T(8,128)(2,1)}, bf16[1024,256]{1,0:T(8,128)(2,1)S(1)}, u32[]{:S(2)}) copy-start(bf16[1024,256]{1,0:T(8,128)(2,1)S(1)} %collective-permute-done.13.refs_1_) | copy-start | bytes 1572868
  301.6 12.8 %collective-permute-start.16 = (bf16[1024,256]{1,0:T(8,128)(2,1)}, bf16[1024,256]{1,0:T(8,128)(2,1)}, u32[]{:S(2)}, u32[]{:S(2)}) collective-permute-start(bf16[1024,256]{1,0:T(8,128)(2,1)} %attend.5.refs_2_), channel_id=1, source_target_pairs={{1,2},{2,1},{5,6},{6,5},{9,10},{10,9},{13,14},{14,13},{17,18},{18,... | collective-permute-start | bytes 1572872 | tf_op jit(solution)/shard_map/ppermute | solution.py:54
  303.1 9.3 %copy-start.9 = (bf16[1024,256]{1,0:T(8,128)(2,1)}, bf16[1024,256]{1,0:T(8,128)(2,1)S(1)}, u32[]{:S(2)}) copy-start(bf16[1024,256]{1,0:T(8,128)(2,1)S(1)} %collective-permute-done.12.refs_2_) | copy-start | bytes 1572868
  303.1 25.5 %collective-permute-start.24 = (bf16[1024,256]{1,0:T(8,128)(2,1)S(1)}, bf16[1024,256]{1,0:T(8,128)(2,1)}, u32[]{:S(2)}, u32[]{:S(2)}) collective-permute-start(bf16[1024,256]{1,0:T(8,128)(2,1)S(1)} %collective-permute-done.12.refs_2_), channel_id=1, source_target_pairs={{1,0},{2,3},{5,4},{6,7},{9,8},{10,11},{13,12},{14,15},{17,16},{18,... | collective-permute-start | bytes 1572872 | tf_op jit(solution)/shard_map/ppermute | solution.py:54
  304.4 13.3 %copy-start.8 = (bf16[1024,256]{1,0:T(8,128)(2,1)}, bf16[1024,256]{1,0:T(8,128)(2,1)S(1)}, u32[]{:S(2)}) copy-start(bf16[1024,256]{1,0:T(8,128)(2,1)S(1)} %collective-permute-done.10.refs_0_) | copy-start | bytes 1572868
  304.4 12.0 %collective-permute-start.14 = (bf16[1024,256]{1,0:T(8,128)(2,1)S(1)}, bf16[1024,256]{1,0:T(8,128)(2,1)S(1)}, u32[]{:S(2)}, u32[]{:S(2)}) collective-permute-start(bf16[1024,256]{1,0:T(8,128)(2,1)S(1)} %collective-permute-done.13.refs_1_), channel_id=1, source_target_pairs={{1,2},{2,1},{5,6},{6,5},{9,10},{10,9},{13,14},{14,13},{17,18},{18,... | collective-permute-start | bytes 1572872 | tf_op jit(solution)/shard_map/ppermute | solution.py:54
  305.2 7.2 %copy-start.11 = (bf16[1024,256]{1,0:T(8,128)(2,1)}, bf16[1024,256]{1,0:T(8,128)(2,1)S(1)}, u32[]{:S(2)}) copy-start(bf16[1024,256]{1,0:T(8,128)(2,1)S(1)} %collective-permute-done.18.refs_1_) | copy-start | bytes 1572868
  314.4 22.5 %collective-permute-start.25 = (bf16[1024,256]{1,0:T(8,128)(2,1)}, bf16[1024,256]{1,0:T(8,128)(2,1)}, u32[]{:S(2)}, u32[]{:S(2)}) collective-permute-start(bf16[1024,256]{1,0:T(8,128)(2,1)} %collective-permute-done.16.refs_4_), channel_id=1, source_target_pairs={{1,0},{2,3},{5,4},{6,7},{9,8},{10,11},{13,12},{14,15},{17,16},{18,... | collective-permute-start | bytes 1572872 | tf_op jit(solution)/shard_map/ppermute | solution.py:54
  315.7 11.6 %collective-permute-start.19 = (bf16[1024,256]{1,0:T(8,128)(2,1)}, bf16[1024,256]{1,0:T(8,128)(2,1)S(1)}, u32[]{:S(2)}, u32[]{:S(2)}) collective-permute-start(bf16[1024,256]{1,0:T(8,128)(2,1)} %collective-permute-done.17.refs_2_), channel_id=1, source_target_pairs={{1,2},{2,1},{5,6},{6,5},{9,10},{10,9},{13,14},{14,13},{17,18},{18,... | collective-permute-start | bytes 1572872 | tf_op jit(solution)/shard_map/ppermute | solution.py:54
  316.4 10.8 %copy-start.13 = (bf16[1024,256]{1,0:T(8,128)(2,1)}, bf16[1024,256]{1,0:T(8,128)(2,1)S(1)}, u32[]{:S(2)}) copy-start(bf16[1024,256]{1,0:T(8,128)(2,1)S(1)} %collective-permute-done.14.refs_2_) | copy-start | bytes 1572868
  316.4 31.6 %collective-permute-start.15 = (bf16[1024,256]{1,0:T(8,128)(2,1)S(1)}, bf16[1024,256]{1,0:T(8,128)(2,1)S(1)}, u32[]{:S(2)}, u32[]{:S(2)}) collective-permute-start(bf16[1024,256]{1,0:T(8,128)(2,1)S(1)} %collective-permute-done.14.refs_2_), channel_id=1, source_target_pairs={{1,0},{2,3},{5,4},{6,7},{9,8},{10,11},{13,12},{14,15},{17,16},{18,... | collective-permute-start | bytes 1572872 | tf_op jit(solution)/shard_map/ppermute | solution.py:54
  317.8 39.5 %collective-permute-start.11 = (bf16[1024,256]{1,0:T(8,128)(2,1)S(1)}, bf16[1024,256]{1,0:T(8,128)(2,1)S(1)}, u32[]{:S(2)}, u32[]{:S(2)}) collective-permute-start(bf16[1024,256]{1,0:T(8,128)(2,1)S(1)} %collective-permute-done.10.refs_0_), channel_id=1, source_target_pairs={{1,0},{2,3},{5,4},{6,7},{9,8},{10,11},{13,12},{14,15},{17,16},{18,... | collective-permute-start | bytes 1572872 | tf_op jit(solution)/shard_map/ppermute | solution.py:54
  327.3 18.1 %copy-start.14 = (bf16[1024,256]{1,0:T(8,128)(2,1)}, bf16[1024,256]{1,0:T(8,128)(2,1)S(1)}, u32[]{:S(2)}) copy-start(bf16[1024,256]{1,0:T(8,128)(2,1)S(1)} %collective-permute-done.19.refs_4_) | copy-start | bytes 1572868
  327.3 35.6 %collective-permute-start.23 = (bf16[1024,256]{1,0:T(8,128)(2,1)S(1)}, bf16[1024,256]{1,0:T(8,128)(2,1)S(1)}, u32[]{:S(2)}, u32[]{:S(2)}) collective-permute-start(bf16[1024,256]{1,0:T(8,128)(2,1)S(1)} %collective-permute-done.19.refs_4_), channel_id=1, source_target_pairs={{1,0},{2,3},{5,4},{6,7},{9,8},{10,11},{13,12},{14,15},{17,16},{18,... | collective-permute-start | bytes 1572872 | tf_op jit(solution)/shard_map/ppermute | solution.py:54
  348.0 14.8 %copy-start.15 = (bf16[1024,256]{1,0:T(8,128)(2,1)}, bf16[1024,256]{1,0:T(8,128)(2,1)S(1)}, u32[]{:S(2)}) copy-start(bf16[1024,256]{1,0:T(8,128)(2,1)S(1)} %collective-permute-done.15.refs_3_) | copy-start | bytes 1572868
  357.2 5.6 %copy-start.16 = (bf16[1024,256]{1,0:T(8,128)(2,1)}, bf16[1024,256]{1,0:T(8,128)(2,1)S(1)}, u32[]{:S(2)}) copy-start(bf16[1024,256]{1,0:T(8,128)(2,1)S(1)} %collective-permute-done.11.refs_1_) | copy-start | bytes 1572868
  362.8 0.8 copy-start.17
Sparse Core Ops, SparseCore 0:
  255.8 58.6 all-gather.1
